TPU v7x, 32 devices: a whole 2x2x4 slice. The times are simulated.
32 devices in a mesh: leaf: 8 (over z, y), front: 4 (over x, core).
Axes of the slice: x: 2, y: 2, z: 4, core: 2. Of those that a mesh axis runs over, the one named last changes fastest.
Arguments:
- leaf_fronts: float32 [8, 1, 2048, 2048], P('leaf', None, 'front'), may hold values from -40 to 40, as said below
- screen_weights: float32 [8, 1, 2048], P('leaf', None, 'front'), may hold values from 0.1 to 2
- parent_tile_index: int32 [8, 1, 12], replicated, may hold values from 0 to 31, as said below
Outputs:
- leaf_panel: float32 [8, 1, 2048, 512], P('leaf', None, 'front')
- parent_panel: float32 [8, 1, 2048, 128], P('leaf', None, 'front')
- parent_update: float32 [8, 1, 2048, 3968], P('leaf', None, 'front')
Inputs may be any that keep to these rules, and one draw needn't show every extreme that they name: `leaf_fronts`: each first-level front is symmetric positive definite. `parent_tile_index`: entry [i, g, a] is the tile of parent (i // 2, g) that receives contribution tile t = 4 * (a // 3) + a % 3 + 1 of front (i, g); tile p covers rows p * 128 to (p + 1) * 128 - 1. The entries of one front are distinct, tile 1 always goes to parent tile 0, and p * 128 // 1024 == t * 128 // 512.
All inputs are finite; a program needn't handle non-finite values.
Results may differ from a plain program's by a relative error of at most 0.00013.
Values sent between devices are 32-bit elements; how exact they have to be, the bound alone decides.
No kernel may reach another device: no remote copies, remote signals or barrier semaphores. Data moves between devices by JAX's collectives and lax.ppermute only.
A program may use at most 128 MiB of HBM per device.

v0:
```python
import functools

import jax
import jax.numpy as jnp
from jax import lax
from jax.experimental import pallas as pl
from jax.experimental.pallas import tpu as pltpu
from jax.sharding import PartitionSpec as P

SEP2 = 1024
PANEL_WIDTH = 128
M2 = 4096
GROUP_TILES = 4
SLAB = 8
GROUP = 32
EXACT = lax.Precision.HIGHEST
VMEM_BYTES = 60 * 2**20

TILE = PANEL_WIDTH
LAST = ((1,), (1,))
PLAIN = ((1,), (0,))
FIRST = ((0,), (0,))


def from_front(value, distance):
    pairs = [(source, source ^ distance) for source in range(lax.axis_size("front"))]
    return lax.ppermute(value, "front", pairs)


def from_sibling(value):
    pairs = [(source, source ^ 1) for source in range(lax.axis_size("leaf"))]
    return lax.ppermute(value, "leaf", pairs)


def after(value, *events):
    return lax.optimization_barrier((value, *events))[0]


def slot_of(offset, count):
    slot, bit, weight = 0, 1, count // 2
    while weight:
        slot = slot + jnp.where((offset & bit) != 0, weight, 0)
        bit, weight = bit * 2, weight // 2
    return slot


def offset_of(slot, count):
    offset, bit, weight = 0, 1, count // 2
    while weight:
        offset += bit if slot & weight else 0
        bit, weight = bit * 2, weight // 2
    return offset


def exact_dot(left, right, contract):
    return lax.dot_general(
        left, right, (contract, ((), ())), precision=EXACT, preferred_element_type=jnp.float32
    )


def plain_dot(left, right):
    return lax.dot_general(left, right, (LAST, ((), ())), preferred_element_type=jnp.float32)


def halves(value):
    high = value.astype(jnp.bfloat16)
    return high, (value - high.astype(jnp.float32)).astype(jnp.bfloat16)


def split_dot(left, right):
    return plain_dot(left[0], right[0]) + (plain_dot(left[0], right[1]) + plain_dot(left[1], right[0]))


def lane(row, index):
    return jnp.broadcast_to(row[:, index : index + 1], row.shape)


def sum_tree(terms):
    while len(terms) > 1:
        terms = [sum(terms[i : i + 2]) for i in range(0, len(terms), 2)]
    return terms[0]


def factor_slab(rows, first, inside, lanes):
    entry = {(i, j): lane(rows[i], first + j) for i in range(SLAB) for j in range(i + 1)}
    rows = [jnp.where(inside, jnp.where(lanes == first + i, 1.0, 0.0), row) for i, row in enumerate(rows)]
    done = []
    for p in range(0, SLAB, 2):
        r = p + 1
        one, mixed, two = entry[p, p], entry[r, p], entry[r, r]
        inverse_one = pl.reciprocal(one, approx=True)
        inverse_two = pl.reciprocal(one * two - mixed * mixed, approx=True) * one
        factor = {i: entry[i, p] * inverse_one for i in range(r, SLAB)}
        rows[r] = rows[r] - factor[r] * rows[p]
        for i in range(p + 2, SLAB):
            entry[i, r] = entry[i, r] - factor[i] * mixed
        for i in range(p + 2, SLAB):
            second = entry[i, r] * inverse_two
            for k in range(p + 2, i + 1):
                entry[i, k] = (entry[i, k] - factor[i] * entry[k, p]) - second * entry[k, r]
            rows[i] = (rows[i] - factor[i] * rows[p]) - second * rows[r]
        done.append(rows[p] * lax.rsqrt(one))
        done.append(rows[r] * (inverse_two * lax.rsqrt(inverse_two)))
    return done


def row_of(q):
    return pl.ds(q, TILE, stride=SLAB)


def clear_rows(a):
    row_ids = lax.broadcasted_iota(jnp.int32, a.shape, 0) & -SLAB
    col_ids = lax.broadcasted_iota(jnp.int32, a.shape, 1) * SLAB
    a[...] = (row_ids == col_ids).astype(jnp.float32)


def factor_steps(a, fronts):
    lanes = lax.broadcasted_iota(jnp.int32, (SLAB, TILE), 1)
    columns = lax.broadcasted_iota(jnp.int32, (TILE, TILE), 1)
    settled = (lax.broadcasted_iota(jnp.int32, (GROUP, TILE), 0) & -SLAB) + SLAB

    def at(i):
        return pl.ds(SLAB * i, SLAB)

    for start in range(0, TILE, GROUP):
        stop = start + GROUP
        rows = [a[at(i), :] for i in range(start, stop)]
        for s in range(0, GROUP, SLAB):
            first = start + s
            inside = (lanes >= first) & (lanes < first + SLAB)
            head = factor_slab(rows[s : s + SLAB], first, inside, lanes)
            for i in range(SLAB):
                a[at(first + i), :] = head[i]
            for i in range(s + SLAB, GROUP):
                terms = [lane(row, start + i) * row for row in head]
                rows[i] = jnp.where(inside, 0.0, rows[i]) - sum_tree(terms)
            if s + SLAB < GROUP:
                yield
        if stop < TILE:
            for q in range(fronts):
                upper = a[pl.ds(SLAB * start + q, GROUP, stride=SLAB), :]
                rest = pl.ds(SLAB * stop + q, TILE - stop, stride=SLAB)
                inverse = jnp.where((columns[:GROUP] >= start + settled) & (columns[:GROUP] < stop), 0.0, upper)
                product = exact_dot(upper, inverse, FIRST)[stop:]
                group = columns[stop:]
                kept = jnp.where((group >= start) & (group < stop), 0.0, a[rest, :])
                a[rest, :] = kept - product
        yield


def factor_blocks(a):
    sublanes = lax.broadcasted_iota(jnp.int32, (SLAB, TILE), 0)
    lanes = lax.broadcasted_iota(jnp.int32, (SLAB, TILE), 1)
    for start in range(0, TILE, SLAB):
        inside = (lanes >= start) & (lanes < start + SLAB)
        block = a[start : start + SLAB, :]
        rows = [jnp.broadcast_to(block[i : i + 1, :], block.shape) for i in range(SLAB)]
        rows = factor_slab(rows, start, inside, lanes)
        for low in range(start + SLAB, TILE, SLAB):
            chosen = sublanes + low
            terms = [jnp.take_along_axis(row, chosen, axis=1) * row for row in rows]
            block = a[low : low + SLAB, :]
            a[low : low + SLAB, :] = jnp.where(inside, 0.0, block) - sum_tree(terms)
        block = rows[0]
        for i in range(1, SLAB):
            block = jnp.where(sublanes == i, rows[i], block)
        a[start : start + SLAB, :] = block
        yield


def place():
    leaf, front = lax.axis_index("leaf"), lax.axis_index("front")
    return leaf, front, leaf & 1


def corner_kernel(*refs, order, first, last, count, devices):
    tiles = order // TILE
    pieces = 2 * devices
    if first == 0:
        slabs, (work, out, heads, a) = refs[:pieces], refs[pieces:]
    else:
        old_work, old_out, out, work, a = refs
    fronts = out.shape[0]
    if first == 0:
        front = place()[1]

        def copy(owner, q, take):
            slot = slot_of(front ^ owner, devices)
            for s in range(devices):

                @pl.when(slot == s)
                def _():
                    take(slabs[q * devices + s])

        for q in range(fronts):
            for e in range(tiles):

                def take_tile(slab):
                    work[q, e * TILE : (e + 1) * TILE, :] = slab[:TILE, :]

                copy(e * GROUP_TILES // count, q, take_tile)

            def take_head(slab):
                heads[q] = slab[TILE:, :]

            copy(0, q, take_head)
    else:
        work[...] = old_work[...]
        out[...] = old_out[...]

    clear_rows(a)

    def step(k, carry):
        block = pl.ds(pl.multiple_of(k * TILE, TILE), TILE)
        for q in range(fronts):
            a[row_of(q), :] = work[q, block, block]
        for _ in factor_steps(a, fronts):
            pass
        kept = lax.broadcasted_iota(jnp.int32, (TILE, TILE), 0) >= lax.broadcasted_iota(jnp.int32, (TILE, TILE), 1)
        for q in range(fronts):
            out[q, block, block] = jnp.where(kept, a[row_of(q), :], 0.0)
        for fixed in range(first, last):

            @pl.when(k == fixed)
            def _():
                here = slice(fixed * TILE, (fixed + 1) * TILE)
                low, rest = slice(0, fixed * TILE), slice((fixed + 1) * TILE, order)
                for q in range(fronts):
                    corner = out[q, here, here]
                    if fixed:
                        chain = exact_dot(work[q, here, low], out[q, low, low], PLAIN)
                        out[q, here, low] = -exact_dot(corner, chain, PLAIN)
                    if fixed + 1 < tiles:
                        out[q, here, rest] = jnp.zeros((TILE, order - (fixed + 1) * TILE), jnp.float32)
                        below = exact_dot(work[q, rest, here], corner, LAST)
                        work[q, rest, here] = below
                        work[q, rest, rest] = work[q, rest, rest] - exact_dot(below, below, LAST)

        return carry

    lax.fori_loop(first, last, step, 0)


def at(tile):
    return pl.ds(pl.multiple_of(tile * TILE, TILE), TILE)


def goal_of(table, i, tile):
    entry = 3 * (tile >> 2) + (tile & 3) - 1
    return jnp.where((tile & 3) == 0, -1, table[place()[0] ^ i, jnp.maximum(entry, 0)])


def panel_of(inverse):
    turned = halves(inverse)
    cut = inverse.shape[0] // 2
    top = tuple(part[:cut, :cut] for part in turned)
    bottom = tuple(part[cut:, :] for part in turned)

    def product(block):
        full = halves(block)
        left = split_dot(tuple(part[:, :cut] for part in full), top)
        return jnp.concatenate([left, split_dot(full, bottom)], axis=1)

    return product


def add_columns(table, i, edges, panel_high, panel_low, column, *, count, skip, devices):
    front = place()[1]
    separator = panel_high.shape[2]
    first = slice((1 - skip) * TILE, (2 - skip) * TILE)
    slot = slot_of(front, devices)
    one = panel_high[slot, first, :], panel_low[slot, first, :]
    for s in range(devices):
        piece = edges[s][:, separator:] - split_dot((panel_high[s], panel_low[s]), one)
        owner = front ^ offset_of(s, devices)
        for t in range(count - skip):
            target = goal_of(table, i, owner * count + skip + t)

            @pl.when(target >= 0)
            def _():
                column[at(target), :] += piece[t * TILE : (t + 1) * TILE, :]


def own_kernel(*refs, count, skip, width, devices):
    table, heads, weights, slab, inverse, fronts_here = refs[:6]
    edges = refs[6 : 6 + devices]
    leaf_panel, column, total, panel_high, panel_low = refs[6 + devices :]
    leaf, front, half = place()
    sent = count - skip
    separator = width // GROUP_TILES
    rows = count * TILE
    first_row = (front * 2 + half) * rows

    total[...] = jnp.zeros_like(total)
    column[...] = jnp.zeros_like(column)
    row_ids = lax.broadcasted_iota(jnp.int32, (TILE, TILE), 0)
    col_ids = lax.broadcasted_iota(jnp.int32, (TILE, TILE), 1)
    near = jnp.where(jnp.abs(row_ids - col_ids) == 1, 1.0, 0.0)
    before = jnp.where((row_ids == 0) & (col_ids == TILE - 1), 1.0, 0.0)
    behind = jnp.where((row_ids == TILE - 1) & (col_ids == 0), 1.0, 0.0)
    first_weights = jnp.where(half == 0, heads[0, 0:1, :TILE], heads[1, 0:1, :TILE])
    column[:TILE, :] = jnp.where(row_ids == col_ids, first_weights + 4.0, 0.0) - near
    column[TILE : 2 * TILE, :] = -before
    inside = first_row < SEP2
    weight = jnp.transpose(jnp.broadcast_to(weights[...], (TILE, rows)))
    for j in range(count):
        mine = (front * 2 + half) * count + j
        line = slice(j * TILE, (j + 1) * TILE)
        total[line, at(mine)] = jnp.where(
            row_ids == col_ids, weight[line, :] + jnp.where(inside, 4.0, 0.0), 0.0
        ) - jnp.where(inside, near, 0.0)

        @pl.when((mine > 0) & inside)
        def _():
            total[line, at(mine - 1)] = -before

        @pl.when((mine + 1) * TILE < SEP2)
        def _():
            total[line, at(mine + 1)] = -behind

    panel_from = panel_of(inverse[0])
    if skip:
        leaf_panel[:TILE, :] = panel_from(slab[:TILE, :])
    for s in range(devices):
        panel = panel_from(edges[s][:, :separator])
        if s == 0:
            leaf_panel[skip * TILE :, :] = panel
        panel_high[s], panel_low[s] = halves(panel)
    add_columns(table, 0, edges, panel_high, panel_low, column, count=count, skip=skip, devices=devices)

    for s in range(devices):
        product = split_dot((panel_high[0], panel_low[0]), (panel_high[s], panel_low[s]))
        for c in range(sent):
            tile = (front ^ offset_of(s, devices)) * count + skip + c
            goal = jnp.maximum(goal_of(table, 0, tile), 0)
            for t in range(sent):
                target = goal_of(table, 0, front * count + skip + t) - (front * 2 + half) * count
                target = jnp.where((target >= 0) & (target < count), target, count)
                line = slice(t * TILE, (t + 1) * TILE)
                source = fronts_here[(skip + t) * TILE : (skip + t + 1) * TILE, at(tile)]
                total[at(target), at(goal)] += source - product[line, c * TILE : (c + 1) * TILE]


def parent_kernel(*refs, count, skip, width, devices):
    table, inverse, column_in, total = refs[:4]
    edges = refs[4 : 4 + devices]
    panel_out, update_out = refs[4 + devices : 6 + devices]
    panel_high, panel_low, column, two_left, two_right, update, a, done = refs[6 + devices :]
    leaf, front, half = place()
    separator = width // GROUP_TILES
    rows = count * TILE
    sent = count - skip
    first_row = pl.multiple_of((front * 2 + half) * rows, TILE)

    column[...] = column_in[...]
    panel_from = panel_of(inverse[1])
    for s in range(devices):
        panel_high[s], panel_low[s] = halves(panel_from(edges[s][:, :separator]))
    add_columns(table, 1, edges, panel_high, panel_low, column, count=count, skip=skip, devices=devices)

    def copy(j):
        line = slice(j * TILE, (j + 1) * TILE)
        update[line, :] = total[line, :]

    def contribution(s):
        product = split_dot((panel_high[0], panel_low[0]), (panel_high[s], panel_low[s]))
        for c in range(sent):
            tile = (front ^ offset_of(s, devices)) * count + skip + c
            goal = jnp.maximum(goal_of(table, 1, tile), 0)
            for t in range(sent):
                target = goal_of(table, 1, front * count + skip + t) - (front * 2 + half) * count
                target = jnp.where((target >= 0) & (target < count), target, count)
                update[at(target), at(goal)] -= product[t * TILE : (t + 1) * TILE, c * TILE : (c + 1) * TILE]

    work = [functools.partial(copy, j) for j in range(count)]
    work += [functools.partial(contribution, s) for s in range(devices)]
    steps, tasks = TILE // SLAB, len(work)
    update[rows:, :] = jnp.zeros_like(update[rows:, :])
    a[...] = column[:TILE, :]
    for k, _ in enumerate(factor_blocks(a)):
        while work and len(work) * steps >= (steps - k) * tasks:
            work.pop(0)()
    for task in work:
        task()
    row_ids = lax.broadcasted_iota(jnp.int32, (TILE, TILE), 0)
    col_ids = lax.broadcasted_iota(jnp.int32, (TILE, TILE), 1)
    turned = halves(jnp.where(row_ids >= col_ids, a[...], 0.0))
    for start in range(0, M2, 1024):
        block = slice(start, start + 1024)
        panel = split_dot(halves(column[block, :]), turned)
        column[block, :] = panel
        high, low = halves(panel)
        two_left[block, :] = jnp.concatenate([high, high, low], axis=1)
        two_right[block, :] = jnp.concatenate([high, low, high], axis=1)
    mine = pl.ds(first_row, rows)
    panel_out[...] = column[mine, :]
    own = two_left[mine, :]
    sends = []
    for start in range(TILE, M2, 512):
        stop = min(start + 512, M2)
        here = slice(start - TILE, stop - TILE)
        update[:rows, start:stop] = update[:rows, start:stop] - plain_dot(own, two_right[start:stop, :])
        send = pltpu.make_async_copy(update.at[:rows, start:stop], update_out.at[:, here], done.at[len(sends)])
        send.start()
        sends.append(send)
    for send in sends:
        send.wait()


def far_kernel(table, *refs, count, skip, devices, cut):
    beyond, (update, out, tiles, got, put) = refs[:2], refs[2:]
    leaf, front, half = place()
    sent = count - skip
    every = [(s, t, c) for s in range(devices) for t in range(sent) for c in range(sent)]

    def place_of(s, t, c):
        tile = (front ^ offset_of(s, devices)) * count + skip + c
        goal = goal_of(table, 1, tile)
        target = goal_of(table, 1, front * count + skip + t) - (front * 2 + half) * count
        valid = (goal > 0) & (target >= 0) & (target < count)
        index = (s * sent + t) * sent + c
        lies = out.at[at(jnp.clip(target, 0, count - 1)), at(jnp.maximum(goal - 1, 0))]
        return tile, index, valid, lies

    def fetch(index, lies):
        return pltpu.make_async_copy(lies, tiles.at[index], got.at[index])

    def store(index, lies):
        return pltpu.make_async_copy(tiles.at[index], lies, put.at[index])

    for s, t, c in every:
        _, index, valid, lies = place_of(s, t, c)

        @pl.when(valid)
        def _():
            fetch(index, lies).start()

    for s, t, c in every:
        tile, index, valid, lies = place_of(s, t, c)
        line = slice(t * TILE, (t + 1) * TILE)
        source = jnp.maximum(tile - (tile >> 2) - 2, 0)

        @pl.when(valid)
        def _():
            fetch(index, lies).wait()

            @pl.when(source < cut)
            def _():
                tiles[index] += beyond[0][line, at(jnp.minimum(source, cut - 1))]

            @pl.when(source >= cut)
            def _():
                tiles[index] += beyond[1][line, at(jnp.maximum(source - cut, 0))]

            store(index, lies).start()

    for s, t, c in every:
        _, index, valid, lies = place_of(s, t, c)

        @pl.when(valid)
        def _():
            store(index, lies).wait()


def slab_kernel(matrix, weights, slab, kept, done, *, chosen):
    copies = [
        pltpu.make_async_copy(
            matrix.at[:TILE, t * TILE : (t + 1) * TILE], slab.at[:TILE, k * TILE : (k + 1) * TILE], done.at[k]
        )
        for k, t in enumerate(chosen)
    ]
    for copy in copies:
        copy.start()
    slab[TILE:, :] = jnp.zeros_like(slab[TILE:, :])
    slab[TILE : TILE + 1, : weights.shape[1]] = weights[...]
    for copy in copies:
        copy.wait()
    kept[...] = slab[...]


def body_kernel(matrix, edge, *refs, skip, chosen, rest):
    parts, done = refs[:-1], refs[-1]
    copies = []
    for target, tiles in ((edge, chosen), *zip(parts, rest)):
        filled = 0
        while filled < len(tiles):
            stop = filled + 1
            while stop < len(tiles) and tiles[stop] == tiles[stop - 1] + 1:
                stop += 1
            copies.append(
                pltpu.make_async_copy(
                    matrix.at[skip * TILE :, tiles[filled] * TILE : (tiles[stop - 1] + 1) * TILE],
                    target.at[:, filled * TILE : stop * TILE],
                    done.at[len(copies)],
                )
            )
            filled = stop
    for copy in copies:
        copy.start()
    for copy in copies:
        copy.wait()


def one_front(matrix, weights, table):
    rows, width = matrix.shape
    devices = lax.axis_size("front")
    count, tiles = rows // TILE, width // TILE
    skip = 1 if count % GROUP_TILES == 0 else 0
    separator = width // GROUP_TILES
    sent = (count - skip) * TILE
    distances = []
    while 2 ** (len(distances) + 1) < devices:
        distances.insert(0, 2 ** (len(distances) + 1))

    def spread(pieces):
        for distance in distances:
            pieces = pieces + [from_front(piece, distance) for piece in pieces]
        return pieces

    vmem = pl.BlockSpec(memory_space=pltpu.VMEM)
    smem = pl.BlockSpec(memory_space=pltpu.SMEM)
    hbm = pl.BlockSpec(memory_space=pl.ANY)
    f32, bf16 = jnp.float32, jnp.bfloat16
    params = pltpu.CompilerParams(vmem_limit_bytes=VMEM_BYTES)
    small = pltpu.CompilerParams(vmem_limit_bytes=VMEM_BYTES // 3)

    corner = list(range(0, tiles, GROUP_TILES))
    rest = [t for t in range(tiles) if t % GROUP_TILES and t != 1]
    slab, kept = pl.pallas_call(
        functools.partial(slab_kernel, chosen=corner),
        out_shape=(jax.ShapeDtypeStruct((TILE + SLAB, separator), f32),) * 2,
        in_specs=[hbm, vmem],
        out_specs=(vmem, vmem),
        scratch_shapes=[pltpu.SemaphoreType.DMA((len(corner),))],
        compiler_params=params,
        cost_estimate=pl.CostEstimate(flops=0, bytes_accessed=2**19, transcendentals=0),
        name="slab",
    )(matrix, weights[None])
    far_slab = from_sibling(slab)
    slabs = spread([slab])
    cut = len(rest) * 3 // 11
    rest = (rest[:cut], rest[cut:])
    edge, *bodies = pl.pallas_call(
        functools.partial(body_kernel, skip=skip, chosen=corner + [1], rest=rest),
        out_shape=(
            jax.ShapeDtypeStruct((sent, (len(corner) + 1) * TILE), f32),
            *(jax.ShapeDtypeStruct((sent, len(part) * TILE), f32) for part in rest),
        ),
        in_specs=[hbm],
        out_specs=(vmem, vmem, vmem),
        scratch_shapes=[pltpu.SemaphoreType.DMA((2 * tiles,))],
        compiler_params=params,
        cost_estimate=pl.CostEstimate(flops=0, bytes_accessed=2**23, transcendentals=0),
        name="body",
    )(after(matrix, slab))
    far_slabs = spread([after(far_slab, edge, *slabs)])
    other_slabs = [from_front(piece, 1) for piece in slabs]
    other_far_slabs = [from_front(piece, 1) for piece in far_slabs]
    far_edge = from_sibling(after(edge, far_slab))
    far = [from_sibling(after(bodies[0], far_slab))]
    near_edges = spread([after(edge, *far_slabs)])

    state = jax.ShapeDtypeStruct((2, separator, separator), f32)
    scratch = pltpu.VMEM((SLAB * TILE, TILE), f32)
    cost = pl.CostEstimate(flops=3 * 10**9, bytes_accessed=2**22, transcendentals=0)
    middle = separator // TILE // 2
    half_kernel = functools.partial(corner_kernel, order=separator, count=count, devices=devices)
    state_one, state_two, heads = pl.pallas_call(
        functools.partial(half_kernel, first=0, last=middle),
        out_shape=(state, state, jax.ShapeDtypeStruct((2, SLAB, separator), f32)),
        in_specs=[vmem] * (2 * devices),
        out_specs=(vmem, vmem, vmem),
        scratch_shapes=[scratch],
        compiler_params=small,
        cost_estimate=cost,
        name="corner_first",
    )(kept, *slabs[1:], *other_slabs, *far_slabs, *other_far_slabs)

    far.append(from_sibling(after(bodies[1], heads)))
    far_edges = spread([after(far_edge, heads)])
    inverse = pl.pallas_call(
        functools.partial(half_kernel, first=middle, last=separator // TILE),
        out_shape=state,
        in_specs=[vmem, vmem],
        out_specs=vmem,
        scratch_shapes=[pltpu.VMEM((2, separator, separator), f32), scratch],
        compiler_params=small,
        cost_estimate=cost,
        name="corner_second",
    )(after(state_one, far_edge), state_two)
    other_edges = [from_front(after(piece, inverse), 1) for piece in near_edges]
    other_far_edges = [from_front(after(piece, inverse), 1) for piece in far_edges]

    sizes = dict(count=count, skip=skip, devices=devices)
    panel_space = pltpu.VMEM((devices, sent, separator), bf16)
    update_shape = jax.ShapeDtypeStruct((rows, M2 - TILE), f32)
    large = pltpu.CompilerParams(vmem_limit_bytes=VMEM_BYTES // 2)
    leaf_panel, column, total = pl.pallas_call(
        functools.partial(own_kernel, width=width, **sizes),
        out_shape=(
            jax.ShapeDtypeStruct((rows, separator), f32),
            jax.ShapeDtypeStruct((M2, TILE), f32),
            jax.ShapeDtypeStruct((rows + TILE, M2), f32),
        ),
        in_specs=[smem] + [vmem] * (5 + devices),
        out_specs=(vmem, vmem, vmem),
        scratch_shapes=[panel_space, panel_space],
        compiler_params=large,
        cost_estimate=pl.CostEstimate(flops=2 * 10**9, bytes_accessed=2**22, transcendentals=0),
        name="own",
    )(table, heads, weights[None], kept, inverse, matrix, *near_edges, *other_edges)
    parent_panel, update = pl.pallas_call(
        functools.partial(parent_kernel, width=width, **sizes),
        out_shape=(jax.ShapeDtypeStruct((rows, TILE), f32), update_shape),
        in_specs=[smem] + [vmem] * (3 + devices),
        out_specs=(vmem, hbm),
        scratch_shapes=[
            panel_space,
            panel_space,
            pltpu.VMEM((M2, TILE), f32),
            pltpu.VMEM((M2, 3 * TILE), bf16),
            pltpu.VMEM((M2, 3 * TILE), bf16),
            pltpu.VMEM((rows + TILE, M2), f32),
            pltpu.VMEM((TILE, TILE), f32),
            pltpu.SemaphoreType.DMA((M2 // 512,)),
        ],
        compiler_params=large,
        cost_estimate=pl.CostEstimate(flops=2 * 10**9, bytes_accessed=2**22, transcendentals=0),
        name="parent",
    )(table, inverse, column, total, *far_edges, *other_far_edges)
    update = pl.pallas_call(
        functools.partial(far_kernel, cut=cut, **sizes),
        out_shape=update_shape,
        in_specs=[smem] + [vmem] * 2 + [hbm],
        out_specs=hbm,
        scratch_shapes=[
            pltpu.VMEM((devices * (count - skip) ** 2, TILE, TILE), f32),
            pltpu.SemaphoreType.DMA((devices * (count - skip) ** 2,)),
            pltpu.SemaphoreType.DMA((devices * (count - skip) ** 2,)),
        ],
        input_output_aliases={3: 0},
        compiler_params=large,
        cost_estimate=pl.CostEstimate(flops=2 * 10**9, bytes_accessed=2**22, transcendentals=0),
        name="far",
    )(table, *far, update)
    return leaf_panel, parent_panel, update


def on_device(leaf_fronts, screen_weights, parent_tile_index):
    results = [
        one_front(leaf_fronts[0, g], screen_weights[0, g], parent_tile_index[:, g])
        for g in range(leaf_fronts.shape[1])
    ]
    return tuple(jnp.stack(parts)[None] for parts in zip(*results))


def solution(mesh):
    in_specs = (P("leaf", None, "front", None), P("leaf", None, "front"), P())
    out_specs = (
        P("leaf", None, "front", None),
        P("leaf", None, "front", None),
        P("leaf", None, "front", None),
    )
    return jax.shard_map(
        on_device, mesh=mesh, in_specs=in_specs, out_specs=out_specs, check_vma=False
    )
```

profile of v0, /device:TPU:0, one launch (start us, length us, event | category | flops | bytes accessed | tf_op | source)
XLA Modules:
  0.0 108.4 jit_solution(14553956010876741564)
XLA Ops:
  0.6 2.5 %slab.1 = (f32[136,512]{1,0:T(8,128)}, f32[136,512]{1,0:T(8,128)}) custom-call(f32[512,2048]{1,0:T(8,128)} %bitcast.6, f32[1,512]{1,0:T(1,128)} %bitcast.12), custom_call_target="tpu_custom_call" | custom-call | bytes 524288 | tf_op jit(solution)/shard_map/slab/pallas_call | solution.py:529
  3.1 3.0 %collective-permute-start.3 = (f32[136,512]{1,0:T(8,128)}, f32[136,512]{1,0:T(8,128)S(1)}, u32[]{:S(2)}, u32[]{:S(2)}) collective-permute-start(f32[136,512]{1,0:T(8,128)} %get-tuple-element.29), channel_id=1, source_target_pairs={{0,4},{4,0},{8,12},{12,8},{16,20},{20,16},{24,28},{28,24},{1,5},{5... | collective-permute-start | bytes 835592 | tf_op jit(solution)/shard_map/ppermute | solution.py:32
  6.2 1.5 %collective-permute-start = (f32[136,512]{1,0:T(8,128)}, f32[136,512]{1,0:T(8,128)S(1)}, u32[]{:S(2)}, u32[]{:S(2)}) collective-permute-start(f32[136,512]{1,0:T(8,128)} %get-tuple-element.29), channel_id=1, source_target_pairs={{0,2},{1,3},{2,0},{3,1},{4,6},{5,7},{6,4},{7,5},{8,10},{9,11},{10,... | collective-permute-start | bytes 835592 | tf_op jit(solution)/shard_map/ppermute | solution.py:27
  7.7 3.9 %body.1 = (f32[384,640]{1,0:T(8,128)}, f32[384,384]{1,0:T(8,128)}, f32[384,1024]{1,0:T(8,128)}) custom-call(f32[512,2048]{1,0:T(8,128)} %bitcast.7), custom_call_target="tpu_custom_call" | custom-call | bytes 8388608 | tf_op jit(solution)/shard_map/body/pallas_call | solution.py:543
  11.6 1.4 %collective-permute-done.3.refs_4_ = f32[136,512]{1,0:T(8,128)S(1)} collective-permute-done((f32[136,512]{1,0:T(8,128)}, f32[136,512]{1,0:T(8,128)S(1)}, u32[]{:S(2)}, u32[]{:S(2)}) %collective-permute-start.3) | collective-permute-done | bytes 278560 | tf_op jit(solution)/shard_map/ppermute | solution.py:32
  13.0 1.7 %collective-permute-start.7 = (f32[384,640]{1,0:T(8,128)}, f32[384,640]{1,0:T(8,128)S(1)}, u32[]{:S(2)}, u32[]{:S(2)}) collective-permute-start(f32[384,640]{1,0:T(8,128)} %get-tuple-element.39.refs_6_), channel_id=1, source_target_pairs={{0,4},{4,0},{8,12},{12,8},{16,20},{20,16},{24,28},{28,24},{1,5},{5... | collective-permute-start | bytes 2949128 | tf_op jit(solution)/shard_map/ppermute | solution.py:32
  14.8 1.5 %collective-permute-start.4 = (f32[136,512]{1,0:T(8,128)S(1)}, f32[136,512]{1,0:T(8,128)S(1)}, u32[]{:S(2)}, u32[]{:S(2)}) collective-permute-start(f32[136,512]{1,0:T(8,128)S(1)} %collective-permute-done.3.refs_4_), channel_id=1, source_target_pairs={{0,2},{1,3},{2,0},{3,1},{4,6},{5,7},{6,4},{7,5},{8,10},{9,11},{10,... | collective-permute-start | bytes 835592 | tf_op jit(solution)/shard_map/ppermute | solution.py:27
  16.3 0.0 collective-permute-start.1
  16.3 0.5 collective-permute-start.5
  16.8 0.0 collective-permute-start.2
  16.8 5.2 %collective-permute-done.4.refs_5_ = f32[136,512]{1,0:T(8,128)S(1)} collective-permute-done((f32[136,512]{1,0:T(8,128)S(1)}, f32[136,512]{1,0:T(8,128)S(1)}, u32[]{:S(2)}, u32[]{:S(2)}) %collective-permute-start.4) | collective-permute-done | bytes 278560 | tf_op jit(solution)/shard_map/ppermute | solution.py:27
  22.0 0.0 collective-permute-start.6
  22.0 0.0 collective-permute-done.1.refs_2_
  22.0 1.5 %collective-permute-start.8 = (f32[384,640]{1,0:T(8,128)}, f32[384,640]{1,0:T(8,128)S(1)}, u32[]{:S(2)}, u32[]{:S(2)}) collective-permute-start(f32[384,640]{1,0:T(8,128)} %get-tuple-element.39.refs_6_), channel_id=1, source_target_pairs={{0,2},{1,3},{2,0},{3,1},{4,6},{5,7},{6,4},{7,5},{8,10},{9,11},{10,... | collective-permute-start | bytes 2949128 | tf_op jit(solution)/shard_map/ppermute | solution.py:27
  23.5 0.0 collective-permute-done.2.refs_3_
  23.5 0.0 collective-permute-done.5.refs_6_
  23.5 0.1 collective-permute-done.6.refs_7_
  23.6 14.9 %corner_first.1 = (f32[2,512,512]{2,1,0:T(8,128)S(1)}, f32[2,512,512]{2,1,0:T(8,128)S(1)}, f32[2,8,512]{2,1,0:T(8,128)S(1)}) custom-call(f32[136,512]{1,0:T(8,128)S(1)} %copy-done.2, f32[136,512]{1,0:T(8,128)S(1)} %collective-permute-done.refs_1_, f32[136,512]{1,0:T(8,128)S(1)} %collective-permute-done.1.refs_2_, ...), custom_call_target="tpu_custom_call" | custom-call | flops 3000000000 | bytes 4194304 | tf_op jit(solution)/shard_map/corner_first/pallas_call | solution.py:568
  38.5 1.6 %collective-permute-start.11 = (f32[384,640]{1,0:T(8,128)S(1)}, f32[384,640]{1,0:T(8,128)S(1)}, u32[]{:S(2)}, u32[]{:S(2)}) collective-permute-start(f32[384,640]{1,0:T(8,128)S(1)} %collective-permute-done.7.refs_4_), channel_id=1, source_target_pairs={{0,2},{1,3},{2,0},{3,1},{4,6},{5,7},{6,4},{7,5},{8,10},{9,11},{10,... | collective-permute-start | bytes 2949128 | tf_op jit(solution)/shard_map/ppermute | solution.py:27
  40.1 0.0 copy-start.3
  40.1 0.0 copy-start.4
  40.1 15.1 %corner_second.1.refs_4_.refs_1_ = f32[2,512,512]{2,1,0:T(8,128)S(1)} custom-call(f32[2,512,512]{2,1,0:T(8,128)S(1)} %get-tuple-element.36.refs_0_, f32[2,512,512]{2,1,0:T(8,128)S(1)} %get-tuple-element.37.refs_1_), custom_call_target="tpu_custom_call" | custom-call | flops 3000000000 | bytes 4194304 | tf_op jit(solution)/shard_map/corner_second/pallas_call | solution.py:581
  55.3 0.1 collective-permute-start.9
  55.3 0.6 collective-permute-start.15
  55.9 0.2 collective-permute-start.10
  56.1 0.4 collective-permute-start.12
  56.4 11.0 %collective-permute-done.11.refs_5_ = f32[384,640]{1,0:T(8,128)S(1)} collective-permute-done((f32[384,640]{1,0:T(8,128)S(1)}, f32[384,640]{1,0:T(8,128)S(1)}, u32[]{:S(2)}, u32[]{:S(2)}) %collective-permute-start.11) | collective-permute-done | bytes 983072 | tf_op jit(solution)/shard_map/ppermute | solution.py:27
  67.5 0.7 collective-permute-start.14
  68.2 11.2 %own.1 = (f32[512,512]{1,0:T(8,128)}, f32[4096,128]{1,0:T(8,128)S(1)}, f32[640,4096]{1,0:T(8,128)S(1)}) custom-call(s32[8,12]{1,0:T(8,128)S(1)} %bitcast.9, f32[2,8,512]{2,1,0:T(8,128)S(1)} %get-tuple-element.33.refs_1_, f32[1,512]{1,0:T(1,128)S(1)} %bitcast.13, f32[136,512]{1,0:T(8,128)S(1)} %copy-done.2, f32[2,512,512]{2,1,0:T(8,128)S(1)} %corner_second.1.refs_4_.refs_1_, ...), custom_call_target="tpu_custom_call" | custom-call | flops 2000000000 | bytes 4194304 | tf_op jit(solution)/shard_map/own/pallas_call | solution.py:598
  79.4 17.1 %parent.1 = (f32[512,128]{1,0:T(8,128)}, f32[512,3968]{1,0:T(8,128)}) custom-call(s32[8,12]{1,0:T(8,128)S(1)} %bitcast.10, f32[2,512,512]{2,1,0:T(8,128)S(1)} %corner_second.1.refs_4_.refs_1_, f32[4096,128]{1,0:T(8,128)S(1)} %get-tuple-element.42.refs_2_, f32[640,4096]{1,0:T(8,128)S(1)} %get-tuple-element.43.refs_3_, ...), custom_call_target="tpu_custom_call" | custom-call | flops 2000000000 | bytes 4194304 | tf_op jit(solution)/shard_map/parent/pallas_call | solution.py:612
  96.4 8.3 %collective-permute-done.14.refs_0_ = f32[384,384]{1,0:T(8,128)S(1)} collective-permute-done((f32[384,384]{1,0:T(8,128)S(1)}, f32[384,384]{1,0:T(8,128)S(1)}, u32[]{:S(2)}, u32[]{:S(2)}) %collective-permute-start.14) | collective-permute-done | bytes 589856 | tf_op jit(solution)/shard_map/ppermute | solution.py:32
  104.8 3.5 %far.1 = f32[512,3968]{1,0:T(8,128)} custom-call(s32[8,12]{1,0:T(8,128)S(1)} %bitcast.11, f32[384,384]{1,0:T(8,128)S(1)} %collective-permute-done.14.refs_0_, f32[384,1024]{1,0:T(8,128)S(1)} %collective-permute-done.15.refs_1_, f32[512,3968]{1,0:T(8,128)} %get-tuple-element.52.refs_2_), custom_call_target="tpu_custom_call", output_to_operand_aliasing={{}: (3, {})} | custom-call | flops 2000000000 | bytes 4194304 | tf_op jit(solution)/shard_map/far/pallas_call | solution.py:631
  (23 shorter events, 0.1 us)
Async XLA Ops:
  3.1 13.2 %copy-start.7 = (f32[136,512]{1,0:T(8,128)S(1)}, f32[136,512]{1,0:T(8,128)}, u32[]{:S(2)}) copy-start(f32[136,512]{1,0:T(8,128)} %get-tuple-element.29) | copy-start | bytes 835588
  3.1 20.5 %copy-start.2 = (f32[136,512]{1,0:T(8,128)S(1)}, f32[136,512]{1,0:T(8,128)}, u32[]{:S(2)}) copy-start(f32[136,512]{1,0:T(8,128)} %get-tuple-element.28.refs_0_.refs_3_) | copy-start | bytes 835588
  3.1 9.9 %collective-permute-start.3 = (f32[136,512]{1,0:T(8,128)}, f32[136,512]{1,0:T(8,128)S(1)}, u32[]{:S(2)}, u32[]{:S(2)}) collective-permute-start(f32[136,512]{1,0:T(8,128)} %get-tuple-element.29), channel_id=1, source_target_pairs={{0,4},{4,0},{8,12},{12,8},{16,20},{20,16},{24,28},{28,24},{1,5},{5... | collective-permute-start | bytes 835592 | tf_op jit(solution)/shard_map/ppermute | solution.py:32
  6.2 8.6 %collective-permute-start = (f32[136,512]{1,0:T(8,128)}, f32[136,512]{1,0:T(8,128)S(1)}, u32[]{:S(2)}, u32[]{:S(2)}) collective-permute-start(f32[136,512]{1,0:T(8,128)} %get-tuple-element.29), channel_id=1, source_target_pairs={{0,2},{1,3},{2,0},{3,1},{4,6},{5,7},{6,4},{7,5},{8,10},{9,11},{10,... | collective-permute-start | bytes 835592 | tf_op jit(solution)/shard_map/ppermute | solution.py:27
  13.0 25.5 %collective-permute-start.7 = (f32[384,640]{1,0:T(8,128)}, f32[384,640]{1,0:T(8,128)S(1)}, u32[]{:S(2)}, u32[]{:S(2)}) collective-permute-start(f32[384,640]{1,0:T(8,128)} %get-tuple-element.39.refs_6_), channel_id=1, source_target_pairs={{0,4},{4,0},{8,12},{12,8},{16,20},{20,16},{24,28},{28,24},{1,5},{5... | collective-permute-start | bytes 2949128 | tf_op jit(solution)/shard_map/ppermute | solution.py:32
  14.8 7.2 %collective-permute-start.4 = (f32[136,512]{1,0:T(8,128)S(1)}, f32[136,512]{1,0:T(8,128)S(1)}, u32[]{:S(2)}, u32[]{:S(2)}) collective-permute-start(f32[136,512]{1,0:T(8,128)S(1)} %collective-permute-done.3.refs_4_), channel_id=1, source_target_pairs={{0,2},{1,3},{2,0},{3,1},{4,6},{5,7},{6,4},{7,5},{8,10},{9,11},{10,... | collective-permute-start | bytes 835592 | tf_op jit(solution)/shard_map/ppermute | solution.py:27
  16.3 5.8 %collective-permute-start.1 = (f32[136,512]{1,0:T(8,128)S(1)}, f32[136,512]{1,0:T(8,128)S(1)}, u32[]{:S(2)}, u32[]{:S(2)}) collective-permute-start(f32[136,512]{1,0:T(8,128)S(1)} %copy-done.7), channel_id=1, source_target_pairs={{0,1},{1,0},{2,3},{3,2},{4,5},{5,4},{6,7},{7,6},{8,9},{9,8},{10,11... | collective-permute-start | bytes 835592 | tf_op jit(solution)/shard_map/ppermute | solution.py:27
  16.3 7.3 %collective-permute-start.5 = (f32[136,512]{1,0:T(8,128)S(1)}, f32[136,512]{1,0:T(8,128)S(1)}, u32[]{:S(2)}, u32[]{:S(2)}) collective-permute-start(f32[136,512]{1,0:T(8,128)S(1)} %collective-permute-done.3.refs_4_), channel_id=1, source_target_pairs={{0,1},{1,0},{2,3},{3,2},{4,5},{5,4},{6,7},{7,6},{8,9},{9,8},{10,11... | collective-permute-start | bytes 835592 | tf_op jit(solution)/shard_map/ppermute | solution.py:27
  16.8 6.7 %collective-permute-start.2 = (f32[136,512]{1,0:T(8,128)S(1)}, f32[136,512]{1,0:T(8,128)S(1)}, u32[]{:S(2)}, u32[]{:S(2)}) collective-permute-start(f32[136,512]{1,0:T(8,128)S(1)} %collective-permute-done.refs_1_), channel_id=1, source_target_pairs={{0,1},{1,0},{2,3},{3,2},{4,5},{5,4},{6,7},{7,6},{8,9},{9,8},{10,11... | collective-permute-start | bytes 835592 | tf_op jit(solution)/shard_map/ppermute | solution.py:27
  22.0 1.6 %collective-permute-start.6 = (f32[136,512]{1,0:T(8,128)S(1)}, f32[136,512]{1,0:T(8,128)S(1)}, u32[]{:S(2)}, u32[]{:S(2)}) collective-permute-start(f32[136,512]{1,0:T(8,128)S(1)} %collective-permute-done.4.refs_5_), channel_id=1, source_target_pairs={{0,1},{1,0},{2,3},{3,2},{4,5},{5,4},{6,7},{7,6},{8,9},{9,8},{10,11... | collective-permute-start | bytes 835592 | tf_op jit(solution)/shard_map/ppermute | solution.py:27
  22.0 33.9 %collective-permute-start.8 = (f32[384,640]{1,0:T(8,128)}, f32[384,640]{1,0:T(8,128)S(1)}, u32[]{:S(2)}, u32[]{:S(2)}) collective-permute-start(f32[384,640]{1,0:T(8,128)} %get-tuple-element.39.refs_6_), channel_id=1, source_target_pairs={{0,2},{1,3},{2,0},{3,1},{4,6},{5,7},{6,4},{7,5},{8,10},{9,11},{10,... | collective-permute-start | bytes 2949128 | tf_op jit(solution)/shard_map/ppermute | solution.py:27
  38.5 28.9 %collective-permute-start.11 = (f32[384,640]{1,0:T(8,128)S(1)}, f32[384,640]{1,0:T(8,128)S(1)}, u32[]{:S(2)}, u32[]{:S(2)}) collective-permute-start(f32[384,640]{1,0:T(8,128)S(1)} %collective-permute-done.7.refs_4_), channel_id=1, source_target_pairs={{0,2},{1,3},{2,0},{3,1},{4,6},{5,7},{6,4},{7,5},{8,10},{9,11},{10,... | collective-permute-start | bytes 2949128 | tf_op jit(solution)/shard_map/ppermute | solution.py:27
  40.1 15.1 %copy-start.1 = (f32[384,640]{1,0:T(8,128)S(1)}, f32[384,640]{1,0:T(8,128)}, u32[]{:S(2)}) copy-start(f32[384,640]{1,0:T(8,128)} %get-tuple-element.39.refs_6_) | copy-start | bytes 2949124
  40.1 15.2 %copy-start.5 = (f32[384,1024]{1,0:T(8,128)S(1)}, f32[384,1024]{1,0:T(8,128)}, u32[]{:S(2)}) copy-start(f32[384,1024]{1,0:T(8,128)} %get-tuple-element.51) | copy-start | bytes 4718596
  40.1 27.4 %copy-start.6 = (f32[384,384]{1,0:T(8,128)S(1)}, f32[384,384]{1,0:T(8,128)}, u32[]{:S(2)}) copy-start(f32[384,384]{1,0:T(8,128)} %get-tuple-element.49) | copy-start | bytes 1769476
  40.1 28.0 %copy-start = (f32[1,1,512,2048]{3,2,1,0:T(8,128)S(1)}, f32[1,1,512,2048]{3,2,1,0:T(8,128)}, u32[]{:S(2)}) copy-start(f32[1,1,512,2048]{3,2,1,0:T(8,128)} %param.3) | copy-start | bytes 12582916
  40.1 28.0 %copy-start.3 = (s32[8,1,12]{2,1,0:T(1,128)S(1)}, s32[8,1,12]{2,1,0:T(1,128)}, u32[]{:S(2)}) copy-start(s32[8,1,12]{2,1,0:T(1,128)} %param.5) | copy-start | bytes 1156
  40.1 28.0 %copy-start.4 = (f32[1,1,512]{2,1,0:T(1,128)S(1)}, f32[1,1,512]{2,1,0:T(1,128)}, u32[]{:S(2)}) copy-start(f32[1,1,512]{2,1,0:T(1,128)} %param.4) | copy-start | bytes 6148
  55.3 12.2 %collective-permute-start.9 = (f32[384,640]{1,0:T(8,128)S(1)}, f32[384,640]{1,0:T(8,128)S(1)}, u32[]{:S(2)}, u32[]{:S(2)}) collective-permute-start(f32[384,640]{1,0:T(8,128)S(1)} %copy-done.1), channel_id=1, source_target_pairs={{0,1},{1,0},{2,3},{3,2},{4,5},{5,4},{6,7},{7,6},{8,9},{9,8},{10,11... | collective-permute-start | bytes 2949128 | tf_op jit(solution)/shard_map/ppermute | solution.py:27
  55.3 49.4 %collective-permute-start.15 = (f32[384,1024]{1,0:T(8,128)S(1)}, f32[384,1024]{1,0:T(8,128)S(1)}, u32[]{:S(2)}, u32[]{:S(2)}) collective-permute-start(f32[384,1024]{1,0:T(8,128)S(1)} %copy-done.5), channel_id=1, source_target_pairs={{0,4},{4,0},{8,12},{12,8},{16,20},{20,16},{24,28},{28,24},{1,5},{5... | collective-permute-start | bytes 4718600 | tf_op jit(solution)/shard_map/ppermute | solution.py:32
  55.9 12.2 %collective-permute-start.10 = (f32[384,640]{1,0:T(8,128)S(1)}, f32[384,640]{1,0:T(8,128)S(1)}, u32[]{:S(2)}, u32[]{:S(2)}) collective-permute-start(f32[384,640]{1,0:T(8,128)S(1)} %collective-permute-done.8.refs_7_), channel_id=1, source_target_pairs={{0,1},{1,0},{2,3},{3,2},{4,5},{5,4},{6,7},{7,6},{8,9},{9,8},{10,11... | collective-permute-start | bytes 2949128 | tf_op jit(solution)/shard_map/ppermute | solution.py:27
  56.1 23.3 %collective-permute-start.12 = (f32[384,640]{1,0:T(8,128)S(1)}, f32[384,640]{1,0:T(8,128)S(1)}, u32[]{:S(2)}, u32[]{:S(2)}) collective-permute-start(f32[384,640]{1,0:T(8,128)S(1)} %collective-permute-done.7.refs_4_), channel_id=1, source_target_pairs={{0,1},{1,0},{2,3},{3,2},{4,5},{5,4},{6,7},{7,6},{8,9},{9,8},{10,11... | collective-permute-start | bytes 2949128 | tf_op jit(solution)/shard_map/ppermute | solution.py:27
  67.5 11.9 %collective-permute-start.13 = (f32[384,640]{1,0:T(8,128)S(1)}, f32[384,640]{1,0:T(8,128)S(1)}, u32[]{:S(2)}, u32[]{:S(2)}) collective-permute-start(f32[384,640]{1,0:T(8,128)S(1)} %collective-permute-done.11.refs_5_), channel_id=1, source_target_pairs={{0,1},{1,0},{2,3},{3,2},{4,5},{5,4},{6,7},{7,6},{8,9},{9,8},{10,11... | collective-permute-start | bytes 2949128 | tf_op jit(solution)/shard_map/ppermute | solution.py:27
  67.5 37.3 %collective-permute-start.14 = (f32[384,384]{1,0:T(8,128)S(1)}, f32[384,384]{1,0:T(8,128)S(1)}, u32[]{:S(2)}, u32[]{:S(2)}) collective-permute-start(f32[384,384]{1,0:T(8,128)S(1)} %copy-done.6), channel_id=1, source_target_pairs={{0,4},{4,0},{8,12},{12,8},{16,20},{20,16},{24,28},{28,24},{1,5},{5... | collective-permute-start | bytes 1769480 | tf_op jit(solution)/shard_map/ppermute | solution.py:32
where the time goes:
time: 109 us; the launch traced here: 108 us
  Pallas kernels  68.2 us (63%)
  waiting for transfers between devices  26.1 us (24%)
  starting transfers between devices  13.2 us (12%)
    pallas_call x1, Pallas kernels, one_front(): pl.pallas_call(functools.partial(parent_kernel, width=width, **sizes), ou...  17.1 us
    ppermute x12, waiting for transfers between devices, from_front(): return lax.ppermute(value, 'front', pairs)  16.3 us
    pallas_call x1, Pallas kernels, one_front(): pl.pallas_call(functools.partial(half_kernel, first=middle, last=separato...  15.1 us
    pallas_call x1, Pallas kernels, one_front(): pl.pallas_call(functools.partial(half_kernel, first=0, last=middle), out_...  14.9 us
    pallas_call x1, Pallas kernels, one_front(): pl.pallas_call(functools.partial(own_kernel, width=width, **sizes), out_s...  11.2 us
    ppermute x4, waiting for transfers between devices, from_sibling(): return lax.ppermute(value, 'leaf', pairs)  9.79 us
    ppermute x12, starting transfers between devices, from_front(): return lax.ppermute(value, 'front', pairs)  7.13 us
    ppermute x4, starting transfers between devices, from_sibling(): return lax.ppermute(value, 'leaf', pairs)  6.02 us
  transfers between devices with their start and end apart: 16, of which 5 were waited for; matrix products, arithmetic and copies ran while one was open for 0% of the time, Pallas kernels for 57%

commit v1 on v0

--- a/solution.py
+++ b/solution.py
@@ -13,6 +13,7 @@
 GROUP_TILES = 4
 SLAB = 8
 GROUP = 32
+STEP = 16
 EXACT = lax.Precision.HIGHEST
 VMEM_BYTES = 60 * 2**20
 
@@ -82,19 +83,20 @@
 
 
 def factor_slab(rows, first, inside, lanes):
-    entry = {(i, j): lane(rows[i], first + j) for i in range(SLAB) for j in range(i + 1)}
+    size = len(rows)
+    entry = {(i, j): lane(rows[i], first + j) for i in range(size) for j in range(i + 1)}
     rows = [jnp.where(inside, jnp.where(lanes == first + i, 1.0, 0.0), row) for i, row in enumerate(rows)]
     done = []
-    for p in range(0, SLAB, 2):
+    for p in range(0, size, 2):
         r = p + 1
         one, mixed, two = entry[p, p], entry[r, p], entry[r, r]
         inverse_one = pl.reciprocal(one, approx=True)
         inverse_two = pl.reciprocal(one * two - mixed * mixed, approx=True) * one
-        factor = {i: entry[i, p] * inverse_one for i in range(r, SLAB)}
+        factor = {i: entry[i, p] * inverse_one for i in range(r, size)}
         rows[r] = rows[r] - factor[r] * rows[p]
-        for i in range(p + 2, SLAB):
+        for i in range(p + 2, size):
             entry[i, r] = entry[i, r] - factor[i] * mixed
-        for i in range(p + 2, SLAB):
+        for i in range(p + 2, size):
             second = entry[i, r] * inverse_two
             for k in range(p + 2, i + 1):
                 entry[i, k] = (entry[i, k] - factor[i] * entry[k, p]) - second * entry[k, r]
@@ -117,7 +119,7 @@
 def factor_steps(a, fronts):
     lanes = lax.broadcasted_iota(jnp.int32, (SLAB, TILE), 1)
     columns = lax.broadcasted_iota(jnp.int32, (TILE, TILE), 1)
-    settled = (lax.broadcasted_iota(jnp.int32, (GROUP, TILE), 0) & -SLAB) + SLAB
+    settled = (lax.broadcasted_iota(jnp.int32, (GROUP, TILE), 0) & -STEP) + STEP
 
     def at(i):
         return pl.ds(SLAB * i, SLAB)
@@ -125,16 +127,16 @@
     for start in range(0, TILE, GROUP):
         stop = start + GROUP
         rows = [a[at(i), :] for i in range(start, stop)]
-        for s in range(0, GROUP, SLAB):
+        for s in range(0, GROUP, STEP):
             first = start + s
-            inside = (lanes >= first) & (lanes < first + SLAB)
-            head = factor_slab(rows[s : s + SLAB], first, inside, lanes)
-            for i in range(SLAB):
+            inside = (lanes >= first) & (lanes < first + STEP)
+            head = factor_slab(rows[s : s + STEP], first, inside, lanes)
+            for i in range(STEP):
                 a[at(first + i), :] = head[i]
-            for i in range(s + SLAB, GROUP):
+            for i in range(s + STEP, GROUP):
                 terms = [lane(row, start + i) * row for row in head]
                 rows[i] = jnp.where(inside, 0.0, rows[i]) - sum_tree(terms)
-            if s + SLAB < GROUP:
+            if s + STEP < GROUP:
                 yield
         if stop < TILE:
             for q in range(fronts):
@@ -407,8 +409,8 @@
         send.wait()
 
 
-def far_kernel(table, *refs, count, skip, devices, cut):
-    beyond, (update, out, tiles, got, put) = refs[:2], refs[2:]
+def far_kernel(table, *refs, count, skip, devices, cuts):
+    beyond, (update, out, tiles, got, put) = refs[: len(cuts) - 1], refs[len(cuts) - 1 :]
     leaf, front, half = place()
     sent = count - skip
     every = [(s, t, c) for s in range(devices) for t in range(sent) for c in range(sent)]
@@ -444,13 +446,11 @@
         def _():
             fetch(index, lies).wait()
 
-            @pl.when(source < cut)
-            def _():
-                tiles[index] += beyond[0][line, at(jnp.minimum(source, cut - 1))]
-
-            @pl.when(source >= cut)
-            def _():
-                tiles[index] += beyond[1][line, at(jnp.maximum(source - cut, 0))]
+            for part, low, high in zip(beyond, cuts, cuts[1:]):
+
+                @pl.when((source >= low) & (source < high))
+                def _():
+                    tiles[index] += part[line, at(jnp.clip(source - low, 0, high - low - 1))]
 
             store(index, lies).start()
 
@@ -538,8 +538,8 @@
     )(matrix, weights[None])
     far_slab = from_sibling(slab)
     slabs = spread([slab])
-    cut = len(rest) * 3 // 11
-    rest = (rest[:cut], rest[cut:])
+    cuts = (0, 1 + len(rest) // 2, len(rest))
+    rest = [rest[low:high] for low, high in zip(cuts, cuts[1:])]
     edge, *bodies = pl.pallas_call(
         functools.partial(body_kernel, skip=skip, chosen=corner + [1], rest=rest),
         out_shape=(
@@ -547,7 +547,7 @@
             *(jax.ShapeDtypeStruct((sent, len(part) * TILE), f32) for part in rest),
         ),
         in_specs=[hbm],
-        out_specs=(vmem, vmem, vmem),
+        out_specs=(vmem,) * (1 + len(rest)),
         scratch_shapes=[pltpu.SemaphoreType.DMA((2 * tiles,))],
         compiler_params=params,
         cost_estimate=pl.CostEstimate(flops=0, bytes_accessed=2**23, transcendentals=0),
@@ -557,7 +557,6 @@
     other_slabs = [from_front(piece, 1) for piece in slabs]
     other_far_slabs = [from_front(piece, 1) for piece in far_slabs]
     far_edge = from_sibling(after(edge, far_slab))
-    far = [from_sibling(after(bodies[0], far_slab))]
     near_edges = spread([after(edge, *far_slabs)])
 
     state = jax.ShapeDtypeStruct((2, separator, separator), f32)
@@ -576,7 +575,7 @@
         name="corner_first",
     )(kept, *slabs[1:], *other_slabs, *far_slabs, *other_far_slabs)
 
-    far.append(from_sibling(after(bodies[1], heads)))
+    far = [from_sibling(after(body, heads)) for body in bodies]
     far_edges = spread([after(far_edge, heads)])
     inverse = pl.pallas_call(
         functools.partial(half_kernel, first=middle, last=separator // TILE),
@@ -608,7 +607,7 @@
         compiler_params=large,
         cost_estimate=pl.CostEstimate(flops=2 * 10**9, bytes_accessed=2**22, transcendentals=0),
         name="own",
-    )(table, heads, weights[None], kept, inverse, matrix, *near_edges, *other_edges)
+    )(table, heads, weights[None], kept, after(inverse, far[0]), matrix, *near_edges, *other_edges)
     parent_panel, update = pl.pallas_call(
         functools.partial(parent_kernel, width=width, **sizes),
         out_shape=(jax.ShapeDtypeStruct((rows, TILE), f32), update_shape),
@@ -629,16 +628,16 @@
         name="parent",
     )(table, inverse, column, total, *far_edges, *other_far_edges)
     update = pl.pallas_call(
-        functools.partial(far_kernel, cut=cut, **sizes),
+        functools.partial(far_kernel, cuts=cuts, **sizes),
         out_shape=update_shape,
-        in_specs=[smem] + [vmem] * 2 + [hbm],
+        in_specs=[smem] + [vmem] * len(far) + [hbm],
         out_specs=hbm,
         scratch_shapes=[
             pltpu.VMEM((devices * (count - skip) ** 2, TILE, TILE), f32),
             pltpu.SemaphoreType.DMA((devices * (count - skip) ** 2,)),
             pltpu.SemaphoreType.DMA((devices * (count - skip) ** 2,)),
         ],
-        input_output_aliases={3: 0},
+        input_output_aliases={1 + len(far): 0},
         compiler_params=large,
         cost_estimate=pl.CostEstimate(flops=2 * 10**9, bytes_accessed=2**22, transcendentals=0),
         name="far",

time: 109 us -> 101 us (0.927)
  waiting for transfers between devices: 26.1 us -> 18.7 us
    ppermute x4, waiting for transfers between devices: 9.79 us -> 1.43 us  [from_sibling(): return lax.ppermute(value, 'leaf', pairs)]
  transfers between devices with their start and end apart: 16 -> 16, of which waited for: 5 -> 4; matrix products, arithmetic and copies ran while one was open for 0% -> 0% of each run, Pallas kernels for 57% -> 61%
where the time goes in v1:
time: 101 us; the launch traced here: 100 us
  Pallas kernels  67.7 us (67%)
  waiting for transfers between devices  18.7 us (19%)
  starting transfers between devices  13.1 us (13%)
    ppermute x12, waiting for transfers between devices, from_front(): return lax.ppermute(value, 'front', pairs)  17.2 us
    pallas_call x1, Pallas kernels, one_front(): pl.pallas_call(functools.partial(parent_kernel, width=width, **sizes), ou...  17.1 us
    pallas_call x1, Pallas kernels, one_front(): pl.pallas_call(functools.partial(half_kernel, first=middle, last=separato...  14.7 us
    pallas_call x1, Pallas kernels, one_front(): pl.pallas_call(functools.partial(half_kernel, first=0, last=middle), out_...  14.5 us
    pallas_call x1, Pallas kernels, one_front(): pl.pallas_call(functools.partial(own_kernel, width=width, **sizes), out_s...  11.2 us
    ppermute x12, starting transfers between devices, from_front(): return lax.ppermute(value, 'front', pairs)  7.03 us
    ppermute x4, starting transfers between devices, from_sibling(): return lax.ppermute(value, 'leaf', pairs)  6.11 us
    pallas_call x1, Pallas kernels, one_front(): pl.pallas_call(functools.partial(body_kernel, skip=skip, chosen=corner +...  3.95 us
  transfers between devices with their start and end apart: 16, of which 4 were waited for; matrix products, arithmetic and copies ran while one was open for 0% of the time, Pallas kernels for 61%

profile of v1, /device:TPU:0, one launch (start us, length us, event | category | flops | bytes accessed | tf_op | source)
XLA Modules:
  0.0 100.5 jit_solution(636240538353286517)
XLA Ops:
  0.6 2.5 %slab.1 = (f32[136,512]{1,0:T(8,128)}, f32[136,512]{1,0:T(8,128)}) custom-call(f32[512,2048]{1,0:T(8,128)} %bitcast.6, f32[1,512]{1,0:T(1,128)} %bitcast.12), custom_call_target="tpu_custom_call" | custom-call | bytes 524288 | tf_op jit(solution)/shard_map/slab/pallas_call | solution.py:529
  3.1 3.0 %collective-permute-start.3 = (f32[136,512]{1,0:T(8,128)}, f32[136,512]{1,0:T(8,128)S(1)}, u32[]{:S(2)}, u32[]{:S(2)}) collective-permute-start(f32[136,512]{1,0:T(8,128)} %get-tuple-element.30), channel_id=1, source_target_pairs={{0,4},{4,0},{8,12},{12,8},{16,20},{20,16},{24,28},{28,24},{1,5},{5... | collective-permute-start | bytes 835592 | tf_op jit(solution)/shard_map/ppermute | solution.py:33
  6.2 1.5 %collective-permute-start = (f32[136,512]{1,0:T(8,128)}, f32[136,512]{1,0:T(8,128)S(1)}, u32[]{:S(2)}, u32[]{:S(2)}) collective-permute-start(f32[136,512]{1,0:T(8,128)} %get-tuple-element.30), channel_id=1, source_target_pairs={{0,2},{1,3},{2,0},{3,1},{4,6},{5,7},{6,4},{7,5},{8,10},{9,11},{10,... | collective-permute-start | bytes 835592 | tf_op jit(solution)/shard_map/ppermute | solution.py:28
  7.7 3.9 %body.1 = (f32[384,640]{1,0:T(8,128)}, f32[384,768]{1,0:T(8,128)}, f32[384,640]{1,0:T(8,128)}) custom-call(f32[512,2048]{1,0:T(8,128)} %bitcast.7), custom_call_target="tpu_custom_call" | custom-call | bytes 8388608 | tf_op jit(solution)/shard_map/body/pallas_call | solution.py:543
  11.6 1.4 %collective-permute-done.3.refs_4_ = f32[136,512]{1,0:T(8,128)S(1)} collective-permute-done((f32[136,512]{1,0:T(8,128)}, f32[136,512]{1,0:T(8,128)S(1)}, u32[]{:S(2)}, u32[]{:S(2)}) %collective-permute-start.3) | collective-permute-done | bytes 278560 | tf_op jit(solution)/shard_map/ppermute | solution.py:33
  13.0 1.7 %collective-permute-start.7 = (f32[384,640]{1,0:T(8,128)}, f32[384,640]{1,0:T(8,128)S(1)}, u32[]{:S(2)}, u32[]{:S(2)}) collective-permute-start(f32[384,640]{1,0:T(8,128)} %get-tuple-element.43.refs_6_), channel_id=1, source_target_pairs={{0,4},{4,0},{8,12},{12,8},{16,20},{20,16},{24,28},{28,24},{1,5},{5... | collective-permute-start | bytes 2949128 | tf_op jit(solution)/shard_map/ppermute | solution.py:33
  14.8 1.5 %collective-permute-start.4 = (f32[136,512]{1,0:T(8,128)S(1)}, f32[136,512]{1,0:T(8,128)S(1)}, u32[]{:S(2)}, u32[]{:S(2)}) collective-permute-start(f32[136,512]{1,0:T(8,128)S(1)} %collective-permute-done.3.refs_4_), channel_id=1, source_target_pairs={{0,2},{1,3},{2,0},{3,1},{4,6},{5,7},{6,4},{7,5},{8,10},{9,11},{10,... | collective-permute-start | bytes 835592 | tf_op jit(solution)/shard_map/ppermute | solution.py:28
  16.3 0.0 collective-permute-start.1
  16.3 0.5 collective-permute-start.5
  16.8 0.0 collective-permute-start.2
  16.8 5.2 %collective-permute-done.4.refs_5_ = f32[136,512]{1,0:T(8,128)S(1)} collective-permute-done((f32[136,512]{1,0:T(8,128)S(1)}, f32[136,512]{1,0:T(8,128)S(1)}, u32[]{:S(2)}, u32[]{:S(2)}) %collective-permute-start.4) | collective-permute-done | bytes 278560 | tf_op jit(solution)/shard_map/ppermute | solution.py:28
  22.0 0.0 collective-permute-start.6
  22.0 0.0 collective-permute-done.1.refs_2_
  22.0 1.5 %collective-permute-start.9 = (f32[384,640]{1,0:T(8,128)}, f32[384,640]{1,0:T(8,128)S(1)}, u32[]{:S(2)}, u32[]{:S(2)}) collective-permute-start(f32[384,640]{1,0:T(8,128)} %get-tuple-element.43.refs_6_), channel_id=1, source_target_pairs={{0,2},{1,3},{2,0},{3,1},{4,6},{5,7},{6,4},{7,5},{8,10},{9,11},{10,... | collective-permute-start | bytes 2949128 | tf_op jit(solution)/shard_map/ppermute | solution.py:28
  23.5 0.0 collective-permute-done.2.refs_3_
  23.5 0.0 collective-permute-done.5.refs_6_
  23.5 0.1 collective-permute-done.6.refs_7_
  23.6 14.5 %corner_first.1 = (f32[2,512,512]{2,1,0:T(8,128)S(1)}, f32[2,512,512]{2,1,0:T(8,128)S(1)}, f32[2,8,512]{2,1,0:T(8,128)S(1)}) custom-call(f32[136,512]{1,0:T(8,128)S(1)} %copy-done.2, f32[136,512]{1,0:T(8,128)S(1)} %collective-permute-done.refs_1_, f32[136,512]{1,0:T(8,128)S(1)} %collective-permute-done.1.refs_2_, ...), custom_call_target="tpu_custom_call" | custom-call | flops 3000000000 | bytes 4194304 | tf_op jit(solution)/shard_map/corner_first/pallas_call | solution.py:567
  38.1 0.7 collective-permute-start.8
  38.8 0.0 collective-permute-done.7.refs_4_
  38.8 1.4 %collective-permute-start.12 = (f32[384,640]{1,0:T(8,128)S(1)}, f32[384,640]{1,0:T(8,128)S(1)}, u32[]{:S(2)}, u32[]{:S(2)}) collective-permute-start(f32[384,640]{1,0:T(8,128)S(1)} %collective-permute-done.7.refs_4_), channel_id=1, source_target_pairs={{0,2},{1,3},{2,0},{3,1},{4,6},{5,7},{6,4},{7,5},{8,10},{9,11},{10,... | collective-permute-start | bytes 2949128 | tf_op jit(solution)/shard_map/ppermute | solution.py:28
  40.2 0.0 copy-start.4
  40.2 14.7 %corner_second.1.refs_4_.refs_1_ = f32[2,512,512]{2,1,0:T(8,128)S(1)} custom-call(f32[2,512,512]{2,1,0:T(8,128)S(1)} %get-tuple-element.37.refs_0_, f32[2,512,512]{2,1,0:T(8,128)S(1)} %get-tuple-element.38.refs_1_), custom_call_target="tpu_custom_call" | custom-call | flops 3000000000 | bytes 4194304 | tf_op jit(solution)/shard_map/corner_second/pallas_call | solution.py:580
  54.9 0.1 collective-permute-start.10
  55.0 0.5 collective-permute-start.11
  55.5 0.1 collective-permute-start.13
  55.5 11.9 %collective-permute-done.12.refs_5_ = f32[384,640]{1,0:T(8,128)S(1)} collective-permute-done((f32[384,640]{1,0:T(8,128)S(1)}, f32[384,640]{1,0:T(8,128)S(1)}, u32[]{:S(2)}, u32[]{:S(2)}) %collective-permute-start.12) | collective-permute-done | bytes 983072 | tf_op jit(solution)/shard_map/ppermute | solution.py:28
  67.5 0.0 collective-permute-start.14
  67.5 0.7 collective-permute-start.15
  68.2 11.2 %own.1 = (f32[512,512]{1,0:T(8,128)}, f32[4096,128]{1,0:T(8,128)S(1)}, f32[640,4096]{1,0:T(8,128)S(1)}) custom-call(s32[8,12]{1,0:T(8,128)S(1)} %bitcast.9, f32[2,8,512]{2,1,0:T(8,128)S(1)} %get-tuple-element.34.refs_1_, f32[1,512]{1,0:T(1,128)S(1)} %bitcast.13, f32[136,512]{1,0:T(8,128)S(1)} %copy-done.2, f32[2,512,512]{2,1,0:T(8,128)S(1)} %corner_second.1.refs_4_.refs_1_, ...), custom_call_target="tpu_custom_call" | custom-call | flops 2000000000 | bytes 4194304 | tf_op jit(solution)/shard_map/own/pallas_call | solution.py:597
  79.4 17.1 %parent.1 = (f32[512,128]{1,0:T(8,128)}, f32[512,3968]{1,0:T(8,128)}) custom-call(s32[8,12]{1,0:T(8,128)S(1)} %bitcast.10, f32[2,512,512]{2,1,0:T(8,128)S(1)} %corner_second.1.refs_4_.refs_1_, f32[4096,128]{1,0:T(8,128)S(1)} %get-tuple-element.46.refs_2_, f32[640,4096]{1,0:T(8,128)S(1)} %get-tuple-element.47.refs_3_, ...), custom_call_target="tpu_custom_call" | custom-call | flops 2000000000 | bytes 4194304 | tf_op jit(solution)/shard_map/parent/pallas_call | solution.py:611
  96.5 3.8 %far.1 = f32[512,3968]{1,0:T(8,128)} custom-call(s32[8,12]{1,0:T(8,128)S(1)} %bitcast.11, f32[384,768]{1,0:T(8,128)S(1)} %collective-permute-done.8.refs_0_, f32[384,640]{1,0:T(8,128)S(1)} %collective-permute-done.15.refs_1_, f32[512,3968]{1,0:T(8,128)} %get-tuple-element.54.refs_2_), custom_call_target="tpu_custom_call", output_to_operand_aliasing={{}: (3, {})} | custom-call | flops 2000000000 | bytes 4194304 | tf_op jit(solution)/shard_map/far/pallas_call | solution.py:630
  (23 shorter events, 0.1 us)
Async XLA Ops:
  3.1 13.2 %copy-start.7 = (f32[136,512]{1,0:T(8,128)S(1)}, f32[136,512]{1,0:T(8,128)}, u32[]{:S(2)}) copy-start(f32[136,512]{1,0:T(8,128)} %get-tuple-element.30) | copy-start | bytes 835588
  3.1 20.5 %copy-start.2 = (f32[136,512]{1,0:T(8,128)S(1)}, f32[136,512]{1,0:T(8,128)}, u32[]{:S(2)}) copy-start(f32[136,512]{1,0:T(8,128)} %get-tuple-element.29.refs_0_.refs_3_) | copy-start | bytes 835588
  3.1 9.9 %collective-permute-start.3 = (f32[136,512]{1,0:T(8,128)}, f32[136,512]{1,0:T(8,128)S(1)}, u32[]{:S(2)}, u32[]{:S(2)}) collective-permute-start(f32[136,512]{1,0:T(8,128)} %get-tuple-element.30), channel_id=1, source_target_pairs={{0,4},{4,0},{8,12},{12,8},{16,20},{20,16},{24,28},{28,24},{1,5},{5... | collective-permute-start | bytes 835592 | tf_op jit(solution)/shard_map/ppermute | solution.py:33
  6.2 8.6 %collective-permute-start = (f32[136,512]{1,0:T(8,128)}, f32[136,512]{1,0:T(8,128)S(1)}, u32[]{:S(2)}, u32[]{:S(2)}) collective-permute-start(f32[136,512]{1,0:T(8,128)} %get-tuple-element.30), channel_id=1, source_target_pairs={{0,2},{1,3},{2,0},{3,1},{4,6},{5,7},{6,4},{7,5},{8,10},{9,11},{10,... | collective-permute-start | bytes 835592 | tf_op jit(solution)/shard_map/ppermute | solution.py:28
  13.0 25.8 %collective-permute-start.7 = (f32[384,640]{1,0:T(8,128)}, f32[384,640]{1,0:T(8,128)S(1)}, u32[]{:S(2)}, u32[]{:S(2)}) collective-permute-start(f32[384,640]{1,0:T(8,128)} %get-tuple-element.43.refs_6_), channel_id=1, source_target_pairs={{0,4},{4,0},{8,12},{12,8},{16,20},{20,16},{24,28},{28,24},{1,5},{5... | collective-permute-start | bytes 2949128 | tf_op jit(solution)/shard_map/ppermute | solution.py:33
  14.8 7.2 %collective-permute-start.4 = (f32[136,512]{1,0:T(8,128)S(1)}, f32[136,512]{1,0:T(8,128)S(1)}, u32[]{:S(2)}, u32[]{:S(2)}) collective-permute-start(f32[136,512]{1,0:T(8,128)S(1)} %collective-permute-done.3.refs_4_), channel_id=1, source_target_pairs={{0,2},{1,3},{2,0},{3,1},{4,6},{5,7},{6,4},{7,5},{8,10},{9,11},{10,... | collective-permute-start | bytes 835592 | tf_op jit(solution)/shard_map/ppermute | solution.py:28
  16.3 5.8 %collective-permute-start.1 = (f32[136,512]{1,0:T(8,128)S(1)}, f32[136,512]{1,0:T(8,128)S(1)}, u32[]{:S(2)}, u32[]{:S(2)}) collective-permute-start(f32[136,512]{1,0:T(8,128)S(1)} %copy-done.7), channel_id=1, source_target_pairs={{0,1},{1,0},{2,3},{3,2},{4,5},{5,4},{6,7},{7,6},{8,9},{9,8},{10,11... | collective-permute-start | bytes 835592 | tf_op jit(solution)/shard_map/ppermute | solution.py:28
  16.3 7.3 %collective-permute-start.5 = (f32[136,512]{1,0:T(8,128)S(1)}, f32[136,512]{1,0:T(8,128)S(1)}, u32[]{:S(2)}, u32[]{:S(2)}) collective-permute-start(f32[136,512]{1,0:T(8,128)S(1)} %collective-permute-done.3.refs_4_), channel_id=1, source_target_pairs={{0,1},{1,0},{2,3},{3,2},{4,5},{5,4},{6,7},{7,6},{8,9},{9,8},{10,11... | collective-permute-start | bytes 835592 | tf_op jit(solution)/shard_map/ppermute | solution.py:28
  16.8 6.7 %collective-permute-start.2 = (f32[136,512]{1,0:T(8,128)S(1)}, f32[136,512]{1,0:T(8,128)S(1)}, u32[]{:S(2)}, u32[]{:S(2)}) collective-permute-start(f32[136,512]{1,0:T(8,128)S(1)} %collective-permute-done.refs_1_), channel_id=1, source_target_pairs={{0,1},{1,0},{2,3},{3,2},{4,5},{5,4},{6,7},{7,6},{8,9},{9,8},{10,11... | collective-permute-start | bytes 835592 | tf_op jit(solution)/shard_map/ppermute | solution.py:28
  22.0 1.6 %collective-permute-start.6 = (f32[136,512]{1,0:T(8,128)S(1)}, f32[136,512]{1,0:T(8,128)S(1)}, u32[]{:S(2)}, u32[]{:S(2)}) collective-permute-start(f32[136,512]{1,0:T(8,128)S(1)} %collective-permute-done.4.refs_5_), channel_id=1, source_target_pairs={{0,1},{1,0},{2,3},{3,2},{4,5},{5,4},{6,7},{7,6},{8,9},{9,8},{10,11... | collective-permute-start | bytes 835592 | tf_op jit(solution)/shard_map/ppermute | solution.py:28
  22.0 32.9 %collective-permute-start.9 = (f32[384,640]{1,0:T(8,128)}, f32[384,640]{1,0:T(8,128)S(1)}, u32[]{:S(2)}, u32[]{:S(2)}) collective-permute-start(f32[384,640]{1,0:T(8,128)} %get-tuple-element.43.refs_6_), channel_id=1, source_target_pairs={{0,2},{1,3},{2,0},{3,1},{4,6},{5,7},{6,4},{7,5},{8,10},{9,11},{10,... | collective-permute-start | bytes 2949128 | tf_op jit(solution)/shard_map/ppermute | solution.py:28
  23.6 14.5 %copy-start.5 = (f32[384,768]{1,0:T(8,128)S(1)}, f32[384,768]{1,0:T(8,128)}, u32[]{:S(2)}) copy-start(f32[384,768]{1,0:T(8,128)} %get-tuple-element.40) | copy-start | bytes 3538948
  38.1 29.4 %collective-permute-start.8 = (f32[384,768]{1,0:T(8,128)S(1)}, f32[384,768]{1,0:T(8,128)S(1)}, u32[]{:S(2)}, u32[]{:S(2)}) collective-permute-start(f32[384,768]{1,0:T(8,128)S(1)} %copy-done.5), channel_id=1, source_target_pairs={{0,4},{4,0},{8,12},{12,8},{16,20},{20,16},{24,28},{28,24},{1,5},{5... | collective-permute-start | bytes 3538952 | tf_op jit(solution)/shard_map/ppermute | solution.py:33
  38.8 28.7 %collective-permute-start.12 = (f32[384,640]{1,0:T(8,128)S(1)}, f32[384,640]{1,0:T(8,128)S(1)}, u32[]{:S(2)}, u32[]{:S(2)}) collective-permute-start(f32[384,640]{1,0:T(8,128)S(1)} %collective-permute-done.7.refs_4_), channel_id=1, source_target_pairs={{0,2},{1,3},{2,0},{3,1},{4,6},{5,7},{6,4},{7,5},{8,10},{9,11},{10,... | collective-permute-start | bytes 2949128 | tf_op jit(solution)/shard_map/ppermute | solution.py:28
  40.2 14.7 %copy-start.1 = (f32[384,640]{1,0:T(8,128)S(1)}, f32[384,640]{1,0:T(8,128)}, u32[]{:S(2)}) copy-start(f32[384,640]{1,0:T(8,128)} %get-tuple-element.43.refs_6_) | copy-start | bytes 2949124
  40.2 27.3 %copy-start.6 = (f32[384,640]{1,0:T(8,128)S(1)}, f32[384,640]{1,0:T(8,128)}, u32[]{:S(2)}) copy-start(f32[384,640]{1,0:T(8,128)} %get-tuple-element.53) | copy-start | bytes 2949124
  40.2 28.0 %copy-start = (f32[1,1,512,2048]{3,2,1,0:T(8,128)S(1)}, f32[1,1,512,2048]{3,2,1,0:T(8,128)}, u32[]{:S(2)}) copy-start(f32[1,1,512,2048]{3,2,1,0:T(8,128)} %param.3) | copy-start | bytes 12582916
  40.2 28.0 %copy-start.3 = (s32[8,1,12]{2,1,0:T(1,128)S(1)}, s32[8,1,12]{2,1,0:T(1,128)}, u32[]{:S(2)}) copy-start(s32[8,1,12]{2,1,0:T(1,128)} %param.5) | copy-start | bytes 1156
  40.2 28.0 %copy-start.4 = (f32[1,1,512]{2,1,0:T(1,128)S(1)}, f32[1,1,512]{2,1,0:T(1,128)}, u32[]{:S(2)}) copy-start(f32[1,1,512]{2,1,0:T(1,128)} %param.4) | copy-start | bytes 6148
  54.9 13.3 %collective-permute-start.10 = (f32[384,640]{1,0:T(8,128)S(1)}, f32[384,640]{1,0:T(8,128)S(1)}, u32[]{:S(2)}, u32[]{:S(2)}) collective-permute-start(f32[384,640]{1,0:T(8,128)S(1)} %copy-done.1), channel_id=1, source_target_pairs={{0,1},{1,0},{2,3},{3,2},{4,5},{5,4},{6,7},{7,6},{8,9},{9,8},{10,11... | collective-permute-start | bytes 2949128 | tf_op jit(solution)/shard_map/ppermute | solution.py:28
  55.0 13.2 %collective-permute-start.11 = (f32[384,640]{1,0:T(8,128)S(1)}, f32[384,640]{1,0:T(8,128)S(1)}, u32[]{:S(2)}, u32[]{:S(2)}) collective-permute-start(f32[384,640]{1,0:T(8,128)S(1)} %collective-permute-done.9.refs_7_), channel_id=1, source_target_pairs={{0,1},{1,0},{2,3},{3,2},{4,5},{5,4},{6,7},{7,6},{8,9},{9,8},{10,11... | collective-permute-start | bytes 2949128 | tf_op jit(solution)/shard_map/ppermute | solution.py:28
  55.5 23.9 %collective-permute-start.13 = (f32[384,640]{1,0:T(8,128)S(1)}, f32[384,640]{1,0:T(8,128)S(1)}, u32[]{:S(2)}, u32[]{:S(2)}) collective-permute-start(f32[384,640]{1,0:T(8,128)S(1)} %collective-permute-done.7.refs_4_), channel_id=1, source_target_pairs={{0,1},{1,0},{2,3},{3,2},{4,5},{5,4},{6,7},{7,6},{8,9},{9,8},{10,11... | collective-permute-start | bytes 2949128 | tf_op jit(solution)/shard_map/ppermute | solution.py:28
  67.5 11.9 %collective-permute-start.14 = (f32[384,640]{1,0:T(8,128)S(1)}, f32[384,640]{1,0:T(8,128)S(1)}, u32[]{:S(2)}, u32[]{:S(2)}) collective-permute-start(f32[384,640]{1,0:T(8,128)S(1)} %collective-permute-done.12.refs_5_), channel_id=1, source_target_pairs={{0,1},{1,0},{2,3},{3,2},{4,5},{5,4},{6,7},{7,6},{8,9},{9,8},{10,11... | collective-permute-start | bytes 2949128 | tf_op jit(solution)/shard_map/ppermute | solution.py:28
  67.5 29.0 %collective-permute-start.15 = (f32[384,640]{1,0:T(8,128)S(1)}, f32[384,640]{1,0:T(8,128)S(1)}, u32[]{:S(2)}, u32[]{:S(2)}) collective-permute-start(f32[384,640]{1,0:T(8,128)S(1)} %copy-done.6), channel_id=1, source_target_pairs={{0,4},{4,0},{8,12},{12,8},{16,20},{20,16},{24,28},{28,24},{1,5},{5... | collective-permute-start | bytes 2949128 | tf_op jit(solution)/shard_map/ppermute | solution.py:33

commit v2 on v1

--- a/solution.py
+++ b/solution.py
@@ -14,7 +14,6 @@
 SLAB = 8
 GROUP = 32
 STEP = 16
-EXACT = lax.Precision.HIGHEST
 VMEM_BYTES = 60 * 2**20
 
 TILE = PANEL_WIDTH
@@ -54,9 +53,16 @@
 
 
 def exact_dot(left, right, contract):
-    return lax.dot_general(
-        left, right, (contract, ((), ())), precision=EXACT, preferred_element_type=jnp.float32
-    )
+    def parts(value):
+        high = value.astype(jnp.bfloat16)
+        value = value - high.astype(jnp.float32)
+        middle = value.astype(jnp.bfloat16)
+        return high, middle, (value - middle.astype(jnp.float32)).astype(jnp.bfloat16)
+
+    left, right = parts(left), parts(right)
+    left = jnp.concatenate([left[k] for k in (0, 0, 1, 0, 1, 2)], axis=contract[0][0])
+    right = jnp.concatenate([right[k] for k in (0, 1, 0, 2, 1, 0)], axis=contract[1][0])
+    return lax.dot_general(left, right, (contract, ((), ())), preferred_element_type=jnp.float32)
 
 
 def plain_dot(left, right):
@@ -478,10 +484,10 @@
     kept[...] = slab[...]
 
 
-def body_kernel(matrix, edge, *refs, skip, chosen, rest):
-    parts, done = refs[:-1], refs[-1]
+def body_kernel(matrix, *refs, skip, wanted):
+    targets, done = refs[:-1], refs[-1]
     copies = []
-    for target, tiles in ((edge, chosen), *zip(parts, rest)):
+    for target, tiles in zip(targets, wanted):
         filled = 0
         while filled < len(tiles):
             stop = filled + 1
@@ -538,17 +544,16 @@
     )(matrix, weights[None])
     far_slab = from_sibling(slab)
     slabs = spread([slab])
-    cuts = (0, 1 + len(rest) // 2, len(rest))
+    cuts = (0, 3, 5, 7, len(rest))
     rest = [rest[low:high] for low, high in zip(cuts, cuts[1:])]
-    edge, *bodies = pl.pallas_call(
-        functools.partial(body_kernel, skip=skip, chosen=corner + [1], rest=rest),
-        out_shape=(
-            jax.ShapeDtypeStruct((sent, (len(corner) + 1) * TILE), f32),
-            *(jax.ShapeDtypeStruct((sent, len(part) * TILE), f32) for part in rest),
-        ),
+    chosen = corner + [1]
+    wanted = [chosen, chosen + rest[0], *rest[1:]]
+    edge, wide, *bodies = pl.pallas_call(
+        functools.partial(body_kernel, skip=skip, wanted=wanted),
+        out_shape=tuple(jax.ShapeDtypeStruct((sent, len(part) * TILE), f32) for part in wanted),
         in_specs=[hbm],
-        out_specs=(vmem,) * (1 + len(rest)),
-        scratch_shapes=[pltpu.SemaphoreType.DMA((2 * tiles,))],
+        out_specs=(vmem,) * len(wanted),
+        scratch_shapes=[pltpu.SemaphoreType.DMA((4 * tiles,))],
         compiler_params=params,
         cost_estimate=pl.CostEstimate(flops=0, bytes_accessed=2**23, transcendentals=0),
         name="body",
@@ -556,13 +561,14 @@
     far_slabs = spread([after(far_slab, edge, *slabs)])
     other_slabs = [from_front(piece, 1) for piece in slabs]
     other_far_slabs = [from_front(piece, 1) for piece in far_slabs]
-    far_edge = from_sibling(after(edge, far_slab))
+    far_wide = from_sibling(after(wide, far_slab))
+    far_edge = far_wide[:, : len(chosen) * TILE]
     near_edges = spread([after(edge, *far_slabs)])
 
     state = jax.ShapeDtypeStruct((2, separator, separator), f32)
     scratch = pltpu.VMEM((SLAB * TILE, TILE), f32)
     cost = pl.CostEstimate(flops=3 * 10**9, bytes_accessed=2**22, transcendentals=0)
-    middle = separator // TILE // 2
+    middle = separator // TILE - 1
     half_kernel = functools.partial(corner_kernel, order=separator, count=count, devices=devices)
     state_one, state_two, heads = pl.pallas_call(
         functools.partial(half_kernel, first=0, last=middle),
@@ -575,7 +581,9 @@
         name="corner_first",
     )(kept, *slabs[1:], *other_slabs, *far_slabs, *other_far_slabs)
 
-    far = [from_sibling(after(body, heads)) for body in bodies]
+    other_edges = [from_front(after(piece, heads), 1) for piece in near_edges]
+    far = [far_wide[:, len(chosen) * TILE :]]
+    far += [from_sibling(after(body, heads)) for body in bodies]
     far_edges = spread([after(far_edge, heads)])
     inverse = pl.pallas_call(
         functools.partial(half_kernel, first=middle, last=separator // TILE),
@@ -586,9 +594,7 @@
         compiler_params=small,
         cost_estimate=cost,
         name="corner_second",
-    )(after(state_one, far_edge), state_two)
-    other_edges = [from_front(after(piece, inverse), 1) for piece in near_edges]
-    other_far_edges = [from_front(after(piece, inverse), 1) for piece in far_edges]
+    )(after(state_one, far_edge, *other_edges), state_two)
 
     sizes = dict(count=count, skip=skip, devices=devices)
     panel_space = pltpu.VMEM((devices, sent, separator), bf16)
@@ -607,7 +613,8 @@
         compiler_params=large,
         cost_estimate=pl.CostEstimate(flops=2 * 10**9, bytes_accessed=2**22, transcendentals=0),
         name="own",
-    )(table, heads, weights[None], kept, after(inverse, far[0]), matrix, *near_edges, *other_edges)
+    )(table, heads, weights[None], kept, after(inverse, far[1]), matrix, *near_edges, *other_edges)
+    other_far_edges = [from_front(after(piece, column, far[2]), 1) for piece in far_edges]
     parent_panel, update = pl.pallas_call(
         functools.partial(parent_kernel, width=width, **sizes),
         out_shape=(jax.ShapeDtypeStruct((rows, TILE), f32), update_shape),

time: 101 us -> 100 us (0.990)
  Pallas kernels: 67.7 us -> 65.3 us
  waiting for transfers between devices: 18.7 us -> 20.2 us
    pallas_call x1, Pallas kernels: 14.7 us -> 5.89 us  [one_front(): pl.pallas_call(functools.partial(half_kernel, first=middle, last=separato...]
    ppermute x4 -> x5, waiting for transfers between devices: 1.43 us -> 8.29 us  [from_sibling(): return lax.ppermute(value, 'leaf', pairs)]
    pallas_call x1, Pallas kernels: 14.5 us -> 20.2 us  [one_front(): pl.pallas_call(functools.partial(half_kernel, first=0, last=middle), out_...]
    ppermute x12, waiting for transfers between devices: 17.2 us -> 11.9 us  [from_front(): return lax.ppermute(value, 'front', pairs)]
    ppermute x4 -> x5, starting transfers between devices: 6.11 us -> 6.24 us  [from_sibling(): return lax.ppermute(value, 'leaf', pairs)]
  transfers between devices with their start and end apart: 16 -> 17, of which waited for: 4 -> 10; matrix products, arithmetic and copies ran while one was open for 0% -> 0% of each run, Pallas kernels for 61% -> 59%
where the time goes in v2:
time: 100 us; the launch traced here: 99.7 us
  Pallas kernels  65.3 us (65%)
  waiting for transfers between devices  20.2 us (20%)
  starting transfers between devices  13.1 us (13%)
    pallas_call x1, Pallas kernels, one_front(): pl.pallas_call(functools.partial(half_kernel, first=0, last=middle), out_...  20.2 us
    pallas_call x1, Pallas kernels, one_front(): pl.pallas_call(functools.partial(parent_kernel, width=width, **sizes), ou...  17.3 us
    ppermute x12, waiting for transfers between devices, from_front(): return lax.ppermute(value, 'front', pairs)  11.9 us
    pallas_call x1, Pallas kernels, one_front(): pl.pallas_call(functools.partial(own_kernel, width=width, **sizes), out_s...  11 us
    ppermute x5, waiting for transfers between devices, from_sibling(): return lax.ppermute(value, 'leaf', pairs)  8.29 us
    ppermute x12, starting transfers between devices, from_front(): return lax.ppermute(value, 'front', pairs)  6.81 us
    ppermute x5, starting transfers between devices, from_sibling(): return lax.ppermute(value, 'leaf', pairs)  6.24 us
    pallas_call x1, Pallas kernels, one_front(): pl.pallas_call(functools.partial(half_kernel, first=middle, last=separato...  5.89 us
  transfers between devices with their start and end apart: 17, of which 10 were waited for; matrix products, arithmetic and copies ran while one was open for 0% of the time, Pallas kernels for 59%

profile of v2, /device:TPU:0, one launch (start us, length us, event | category | flops | bytes accessed | tf_op | source)
XLA Modules:
  0.0 99.7 jit_solution(13232526197645527140)
XLA Ops:
  0.6 2.5 %slab.1 = (f32[136,512]{1,0:T(8,128)}, f32[136,512]{1,0:T(8,128)}) custom-call(f32[512,2048]{1,0:T(8,128)} %bitcast.6, f32[1,512]{1,0:T(1,128)} %bitcast.12), custom_call_target="tpu_custom_call" | custom-call | bytes 524288 | tf_op jit(solution)/shard_map/slab/pallas_call | solution.py:535
  3.1 3.0 %collective-permute-start.3 = (f32[136,512]{1,0:T(8,128)}, f32[136,512]{1,0:T(8,128)S(1)}, u32[]{:S(2)}, u32[]{:S(2)}) collective-permute-start(f32[136,512]{1,0:T(8,128)} %get-tuple-element.33), channel_id=1, source_target_pairs={{0,4},{4,0},{8,12},{12,8},{16,20},{20,16},{24,28},{28,24},{1,5},{5... | collective-permute-start | bytes 835592 | tf_op jit(solution)/shard_map/ppermute | solution.py:32
  6.2 1.5 %collective-permute-start = (f32[136,512]{1,0:T(8,128)}, f32[136,512]{1,0:T(8,128)S(1)}, u32[]{:S(2)}, u32[]{:S(2)}) collective-permute-start(f32[136,512]{1,0:T(8,128)} %get-tuple-element.33), channel_id=1, source_target_pairs={{0,2},{1,3},{2,0},{3,1},{4,6},{5,7},{6,4},{7,5},{8,10},{9,11},{10,... | collective-permute-start | bytes 835592 | tf_op jit(solution)/shard_map/ppermute | solution.py:27
  7.6 4.9 %body.1 = (f32[384,640]{1,0:T(8,128)}, f32[384,1024]{1,0:T(8,128)}, f32[384,256]{1,0:T(8,128)}, f32[384,256]{1,0:T(8,128)}, f32[384,512]{1,0:T(8,128)}) custom-call(f32[512,2048]{1,0:T(8,128)} %bitcast.7), custom_call_target="tpu_custom_call" | custom-call | bytes 8388608 | tf_op jit(solution)/shard_map/body/pallas_call | solution.py:551
  12.5 0.5 collective-permute-done.3.refs_4_
  13.0 1.5 %collective-permute-done.refs_1_ = f32[136,512]{1,0:T(8,128)S(1)} collective-permute-done((f32[136,512]{1,0:T(8,128)}, f32[136,512]{1,0:T(8,128)S(1)}, u32[]{:S(2)}, u32[]{:S(2)}) %collective-permute-start) | collective-permute-done | bytes 278560 | tf_op jit(solution)/shard_map/ppermute | solution.py:27
  14.5 1.5 %collective-permute-start.4 = (f32[136,512]{1,0:T(8,128)S(1)}, f32[136,512]{1,0:T(8,128)S(1)}, u32[]{:S(2)}, u32[]{:S(2)}) collective-permute-start(f32[136,512]{1,0:T(8,128)S(1)} %collective-permute-done.3.refs_4_), channel_id=1, source_target_pairs={{0,2},{1,3},{2,0},{3,1},{4,6},{5,7},{6,4},{7,5},{8,10},{9,11},{10,... | collective-permute-start | bytes 835592 | tf_op jit(solution)/shard_map/ppermute | solution.py:27
  16.0 0.5 collective-permute-start.7
  16.5 5.2 %collective-permute-done.4.refs_5_ = f32[136,512]{1,0:T(8,128)S(1)} collective-permute-done((f32[136,512]{1,0:T(8,128)S(1)}, f32[136,512]{1,0:T(8,128)S(1)}, u32[]{:S(2)}, u32[]{:S(2)}) %collective-permute-start.4) | collective-permute-done | bytes 278560 | tf_op jit(solution)/shard_map/ppermute | solution.py:27
  21.7 1.5 %collective-permute-start.9 = (f32[384,640]{1,0:T(8,128)}, f32[384,640]{1,0:T(8,128)S(1)}, u32[]{:S(2)}, u32[]{:S(2)}) collective-permute-start(f32[384,640]{1,0:T(8,128)} %get-tuple-element.42.refs_6_), channel_id=1, source_target_pairs={{0,2},{1,3},{2,0},{3,1},{4,6},{5,7},{6,4},{7,5},{8,10},{9,11},{10,... | collective-permute-start | bytes 2949128 | tf_op jit(solution)/shard_map/ppermute | solution.py:27
  23.2 0.5 collective-permute-start.5
  23.7 1.0 %collective-permute-done.1.refs_2_ = f32[136,512]{1,0:T(8,128)S(1)} collective-permute-done((f32[136,512]{1,0:T(8,128)S(1)}, f32[136,512]{1,0:T(8,128)S(1)}, u32[]{:S(2)}, u32[]{:S(2)}) %collective-permute-start.1) | collective-permute-done | bytes 278560 | tf_op jit(solution)/shard_map/ppermute | solution.py:27
  24.7 0.1 collective-permute-start.6
  24.9 0.7 collective-permute-done.2.refs_3_
  25.5 0.8 collective-permute-done.6.refs_7_
  26.3 20.2 %corner_first.1 = (f32[2,512,512]{2,1,0:T(8,128)S(1)}, f32[2,512,512]{2,1,0:T(8,128)S(1)}, f32[2,8,512]{2,1,0:T(8,128)S(1)}) custom-call(f32[136,512]{1,0:T(8,128)S(1)} %copy-done.2, f32[136,512]{1,0:T(8,128)S(1)} %collective-permute-done.refs_1_, f32[136,512]{1,0:T(8,128)S(1)} %collective-permute-done.1.refs_2_, ...), custom_call_target="tpu_custom_call" | custom-call | flops 3000000000 | bytes 4194304 | tf_op jit(solution)/shard_map/corner_first/pallas_call | solution.py:573
  46.6 0.2 collective-permute-start.8
  46.8 0.4 collective-permute-start.10
  47.2 3.7 %collective-permute-done.7 = f32[384,1024]{1,0:T(8,128)S(1)} collective-permute-done((f32[384,1024]{1,0:T(8,128)}, f32[384,1024]{1,0:T(8,128)S(1)}, u32[]{:S(2)}, u32[]{:S(2)}) %collective-permute-start.7) | collective-permute-done | bytes 1572896 | tf_op jit(solution)/shard_map/ppermute | solution.py:32
  50.9 0.1 slice.8.refs_4_
  50.9 0.6 collective-permute-start.12
  51.5 0.7 collective-permute-start.11
  52.2 1.4 %collective-permute-start.13 = (f32[384,256]{1,0:T(8,128)S(1)}, f32[384,256]{1,0:T(8,128)S(1)}, u32[]{:S(2)}, u32[]{:S(2)}) collective-permute-start(f32[384,256]{1,0:T(8,128)S(1)} %copy-done.6), channel_id=1, source_target_pairs={{0,4},{4,0},{8,12},{12,8},{16,20},{20,16},{24,28},{28,24},{1,5},{5... | collective-permute-start | bytes 1179656 | tf_op jit(solution)/shard_map/ppermute | solution.py:32
  53.6 5.9 %corner_second.1.refs_4_.refs_1_ = f32[2,512,512]{2,1,0:T(8,128)S(1)} custom-call(f32[2,512,512]{2,1,0:T(8,128)S(1)} %get-tuple-element.44.refs_0_, f32[2,512,512]{2,1,0:T(8,128)S(1)} %get-tuple-element.45.refs_1_), custom_call_target="tpu_custom_call" | custom-call | flops 3000000000 | bytes 4194304 | tf_op jit(solution)/shard_map/corner_second/pallas_call | solution.py:588
  59.5 4.1 %collective-permute-done.11.refs_1_ = f32[384,256]{1,0:T(8,128)S(1)} collective-permute-done((f32[384,256]{1,0:T(8,128)S(1)}, f32[384,256]{1,0:T(8,128)S(1)}, u32[]{:S(2)}, u32[]{:S(2)}) %collective-permute-start.11) | collective-permute-done | bytes 393248 | tf_op jit(solution)/shard_map/ppermute | solution.py:32
  63.6 11.0 %own.1 = (f32[512,512]{1,0:T(8,128)}, f32[4096,128]{1,0:T(8,128)S(1)}, f32[640,4096]{1,0:T(8,128)S(1)}) custom-call(s32[8,12]{1,0:T(8,128)S(1)} %bitcast.9, f32[2,8,512]{2,1,0:T(8,128)S(1)} %get-tuple-element.37.refs_1_, f32[1,512]{1,0:T(1,128)S(1)} %bitcast.13, f32[136,512]{1,0:T(8,128)S(1)} %copy-done.2, f32[2,512,512]{2,1,0:T(8,128)S(1)} %corner_second.1.refs_4_.refs_1_, ...), custom_call_target="tpu_custom_call" | custom-call | flops 2000000000 | bytes 4194304 | tf_op jit(solution)/shard_map/own/pallas_call | solution.py:603
  74.6 0.5 collective-permute-start.15
  75.1 0.7 collective-permute-start.16
  75.9 1.3 %collective-permute-done.14.refs_6_ = f32[384,640]{1,0:T(8,128)S(1)} collective-permute-done((f32[384,640]{1,0:T(8,128)S(1)}, f32[384,640]{1,0:T(8,128)S(1)}, u32[]{:S(2)}, u32[]{:S(2)}) %collective-permute-start.14) | collective-permute-done | bytes 983072 | tf_op jit(solution)/shard_map/ppermute | solution.py:27
  77.2 1.4 %collective-permute-done.15.refs_7_ = f32[384,640]{1,0:T(8,128)S(1)} collective-permute-done((f32[384,640]{1,0:T(8,128)S(1)}, f32[384,640]{1,0:T(8,128)S(1)}, u32[]{:S(2)}, u32[]{:S(2)}) %collective-permute-start.15) | collective-permute-done | bytes 983072 | tf_op jit(solution)/shard_map/ppermute | solution.py:27
  78.6 17.3 %parent.1 = (f32[512,128]{1,0:T(8,128)}, f32[512,3968]{1,0:T(8,128)}) custom-call(s32[8,12]{1,0:T(8,128)S(1)} %bitcast.10, f32[2,512,512]{2,1,0:T(8,128)S(1)} %corner_second.1.refs_4_.refs_1_, f32[4096,128]{1,0:T(8,128)S(1)} %get-tuple-element.50.refs_2_, f32[640,4096]{1,0:T(8,128)S(1)} %get-tuple-element.51.refs_3_, f32[384,640]{1,0:T(8,128)S(1)} %slice.8.refs_4_, ...), custom_call_target="tpu_custom_call" | custom-call | flops 2000000000 | bytes 4194304 | tf_op jit(solution)/shard_map/parent/pallas_call | solution.py:618
  95.9 3.6 %far.1 = f32[512,3968]{1,0:T(8,128)} custom-call(s32[8,12]{1,0:T(8,128)S(1)} %bitcast.11, f32[384,384]{1,0:T(8,128)S(1)} %slice.9.refs_0_, f32[384,256]{1,0:T(8,128)S(1)} %collective-permute-done.11.refs_1_, f32[384,256]{1,0:T(8,128)S(1)} %collective-permute-done.13.refs_2_, ...), custom_call_target="tpu_custom_call", output_to_operand_aliasing={{}: (5, {})} | custom-call | flops 2000000000 | bytes 4194304 | tf_op jit(solution)/shard_map/far/pallas_call | solution.py:637
  (29 shorter events, 0.1 us)
Async XLA Ops:
  3.1 20.1 %copy-start.8 = (f32[136,512]{1,0:T(8,128)S(1)}, f32[136,512]{1,0:T(8,128)}, u32[]{:S(2)}) copy-start(f32[136,512]{1,0:T(8,128)} %get-tuple-element.33) | copy-start | bytes 835588
  3.1 23.2 %copy-start.2 = (f32[136,512]{1,0:T(8,128)S(1)}, f32[136,512]{1,0:T(8,128)}, u32[]{:S(2)}) copy-start(f32[136,512]{1,0:T(8,128)} %get-tuple-element.32.refs_0_.refs_3_) | copy-start | bytes 835588
  3.1 9.9 %collective-permute-start.3 = (f32[136,512]{1,0:T(8,128)}, f32[136,512]{1,0:T(8,128)S(1)}, u32[]{:S(2)}, u32[]{:S(2)}) collective-permute-start(f32[136,512]{1,0:T(8,128)} %get-tuple-element.33), channel_id=1, source_target_pairs={{0,4},{4,0},{8,12},{12,8},{16,20},{20,16},{24,28},{28,24},{1,5},{5... | collective-permute-start | bytes 835592 | tf_op jit(solution)/shard_map/ppermute | solution.py:32
  6.2 8.3 %collective-permute-start = (f32[136,512]{1,0:T(8,128)}, f32[136,512]{1,0:T(8,128)S(1)}, u32[]{:S(2)}, u32[]{:S(2)}) collective-permute-start(f32[136,512]{1,0:T(8,128)} %get-tuple-element.33), channel_id=1, source_target_pairs={{0,2},{1,3},{2,0},{3,1},{4,6},{5,7},{6,4},{7,5},{8,10},{9,11},{10,... | collective-permute-start | bytes 835592 | tf_op jit(solution)/shard_map/ppermute | solution.py:27
  14.5 7.2 %collective-permute-start.4 = (f32[136,512]{1,0:T(8,128)S(1)}, f32[136,512]{1,0:T(8,128)S(1)}, u32[]{:S(2)}, u32[]{:S(2)}) collective-permute-start(f32[136,512]{1,0:T(8,128)S(1)} %collective-permute-done.3.refs_4_), channel_id=1, source_target_pairs={{0,2},{1,3},{2,0},{3,1},{4,6},{5,7},{6,4},{7,5},{8,10},{9,11},{10,... | collective-permute-start | bytes 835592 | tf_op jit(solution)/shard_map/ppermute | solution.py:27
  16.0 34.9 %collective-permute-start.7 = (f32[384,1024]{1,0:T(8,128)}, f32[384,1024]{1,0:T(8,128)S(1)}, u32[]{:S(2)}, u32[]{:S(2)}) collective-permute-start(f32[384,1024]{1,0:T(8,128)} %get-tuple-element.40), channel_id=1, source_target_pairs={{0,4},{4,0},{8,12},{12,8},{16,20},{20,16},{24,28},{28,24},{1,5},{5... | collective-permute-start | bytes 4718600 | tf_op jit(solution)/shard_map/ppermute | solution.py:32
  21.7 25.1 %collective-permute-start.9 = (f32[384,640]{1,0:T(8,128)}, f32[384,640]{1,0:T(8,128)S(1)}, u32[]{:S(2)}, u32[]{:S(2)}) collective-permute-start(f32[384,640]{1,0:T(8,128)} %get-tuple-element.42.refs_6_), channel_id=1, source_target_pairs={{0,2},{1,3},{2,0},{3,1},{4,6},{5,7},{6,4},{7,5},{8,10},{9,11},{10,... | collective-permute-start | bytes 2949128 | tf_op jit(solution)/shard_map/ppermute | solution.py:27
  23.2 1.6 %collective-permute-start.1 = (f32[136,512]{1,0:T(8,128)S(1)}, f32[136,512]{1,0:T(8,128)S(1)}, u32[]{:S(2)}, u32[]{:S(2)}) collective-permute-start(f32[136,512]{1,0:T(8,128)S(1)} %copy-done.8), channel_id=1, source_target_pairs={{0,1},{1,0},{2,3},{3,2},{4,5},{5,4},{6,7},{7,6},{8,9},{9,8},{10,11... | collective-permute-start | bytes 835592 | tf_op jit(solution)/shard_map/ppermute | solution.py:27
  23.2 2.4 %collective-permute-start.5 = (f32[136,512]{1,0:T(8,128)S(1)}, f32[136,512]{1,0:T(8,128)S(1)}, u32[]{:S(2)}, u32[]{:S(2)}) collective-permute-start(f32[136,512]{1,0:T(8,128)S(1)} %collective-permute-done.3.refs_4_), channel_id=1, source_target_pairs={{0,1},{1,0},{2,3},{3,2},{4,5},{5,4},{6,7},{7,6},{8,9},{9,8},{10,11... | collective-permute-start | bytes 835592 | tf_op jit(solution)/shard_map/ppermute | solution.py:27
  23.7 1.8 %collective-permute-start.2 = (f32[136,512]{1,0:T(8,128)S(1)}, f32[136,512]{1,0:T(8,128)S(1)}, u32[]{:S(2)}, u32[]{:S(2)}) collective-permute-start(f32[136,512]{1,0:T(8,128)S(1)} %collective-permute-done.refs_1_), channel_id=1, source_target_pairs={{0,1},{1,0},{2,3},{3,2},{4,5},{5,4},{6,7},{7,6},{8,9},{9,8},{10,11... | collective-permute-start | bytes 835592 | tf_op jit(solution)/shard_map/ppermute | solution.py:27
  24.7 1.6 %collective-permute-start.6 = (f32[136,512]{1,0:T(8,128)S(1)}, f32[136,512]{1,0:T(8,128)S(1)}, u32[]{:S(2)}, u32[]{:S(2)}) collective-permute-start(f32[136,512]{1,0:T(8,128)S(1)} %collective-permute-done.4.refs_5_), channel_id=1, source_target_pairs={{0,1},{1,0},{2,3},{3,2},{4,5},{5,4},{6,7},{7,6},{8,9},{9,8},{10,11... | collective-permute-start | bytes 835592 | tf_op jit(solution)/shard_map/ppermute | solution.py:27
  26.3 20.3 %copy-start.1 = (f32[384,640]{1,0:T(8,128)S(1)}, f32[384,640]{1,0:T(8,128)}, u32[]{:S(2)}) copy-start(f32[384,640]{1,0:T(8,128)} %get-tuple-element.42.refs_6_) | copy-start | bytes 2949124
  26.3 25.2 %copy-start.7 = (f32[384,256]{1,0:T(8,128)S(1)}, f32[384,256]{1,0:T(8,128)}, u32[]{:S(2)}) copy-start(f32[384,256]{1,0:T(8,128)} %get-tuple-element.47) | copy-start | bytes 1179652
  26.3 25.9 %copy-start.6 = (f32[384,256]{1,0:T(8,128)S(1)}, f32[384,256]{1,0:T(8,128)}, u32[]{:S(2)}) copy-start(f32[384,256]{1,0:T(8,128)} %get-tuple-element.54) | copy-start | bytes 1179652
  46.6 7.0 %collective-permute-start.8 = (f32[384,640]{1,0:T(8,128)S(1)}, f32[384,640]{1,0:T(8,128)S(1)}, u32[]{:S(2)}, u32[]{:S(2)}) collective-permute-start(f32[384,640]{1,0:T(8,128)S(1)} %copy-done.1), channel_id=1, source_target_pairs={{0,1},{1,0},{2,3},{3,2},{4,5},{5,4},{6,7},{7,6},{8,9},{9,8},{10,11... | collective-permute-start | bytes 2949128 | tf_op jit(solution)/shard_map/ppermute | solution.py:27
  46.8 6.8 %collective-permute-start.10 = (f32[384,640]{1,0:T(8,128)S(1)}, f32[384,640]{1,0:T(8,128)S(1)}, u32[]{:S(2)}, u32[]{:S(2)}) collective-permute-start(f32[384,640]{1,0:T(8,128)S(1)} %collective-permute-done.9.refs_7_), channel_id=1, source_target_pairs={{0,1},{1,0},{2,3},{3,2},{4,5},{5,4},{6,7},{7,6},{8,9},{9,8},{10,11... | collective-permute-start | bytes 2949128 | tf_op jit(solution)/shard_map/ppermute | solution.py:27
  50.9 23.7 %collective-permute-start.12 = (f32[384,640]{1,0:T(8,128)S(1)}, f32[384,640]{1,0:T(8,128)S(1)}, u32[]{:S(2)}, u32[]{:S(2)}) collective-permute-start(f32[384,640]{1,0:T(8,128)S(1)} %slice.8.refs_4_), channel_id=1, source_target_pairs={{0,2},{1,3},{2,0},{3,1},{4,6},{5,7},{6,4},{7,5},{8,10},{9,11},{10,... | collective-permute-start | bytes 2949128 | tf_op jit(solution)/shard_map/ppermute | solution.py:27
  51.5 12.1 %collective-permute-start.11 = (f32[384,256]{1,0:T(8,128)S(1)}, f32[384,256]{1,0:T(8,128)S(1)}, u32[]{:S(2)}, u32[]{:S(2)}) collective-permute-start(f32[384,256]{1,0:T(8,128)S(1)} %copy-done.7), channel_id=1, source_target_pairs={{0,4},{4,0},{8,12},{12,8},{16,20},{20,16},{24,28},{28,24},{1,5},{5... | collective-permute-start | bytes 1179656 | tf_op jit(solution)/shard_map/ppermute | solution.py:32
  52.2 22.4 %collective-permute-start.13 = (f32[384,256]{1,0:T(8,128)S(1)}, f32[384,256]{1,0:T(8,128)S(1)}, u32[]{:S(2)}, u32[]{:S(2)}) collective-permute-start(f32[384,256]{1,0:T(8,128)S(1)} %copy-done.6), channel_id=1, source_target_pairs={{0,4},{4,0},{8,12},{12,8},{16,20},{20,16},{24,28},{28,24},{1,5},{5... | collective-permute-start | bytes 1179656 | tf_op jit(solution)/shard_map/ppermute | solution.py:32
  53.6 10.0 %copy-start = (f32[1,1,512,2048]{3,2,1,0:T(8,128)S(1)}, f32[1,1,512,2048]{3,2,1,0:T(8,128)}, u32[]{:S(2)}) copy-start(f32[1,1,512,2048]{3,2,1,0:T(8,128)} %param.3) | copy-start | bytes 12582916
  53.6 10.0 %copy-start.3 = (s32[8,1,12]{2,1,0:T(1,128)S(1)}, s32[8,1,12]{2,1,0:T(1,128)}, u32[]{:S(2)}) copy-start(s32[8,1,12]{2,1,0:T(1,128)} %param.5) | copy-start | bytes 1156
  53.6 10.0 %copy-start.4 = (f32[1,1,512]{2,1,0:T(1,128)S(1)}, f32[1,1,512]{2,1,0:T(1,128)}, u32[]{:S(2)}) copy-start(f32[1,1,512]{2,1,0:T(1,128)} %param.4) | copy-start | bytes 6148
  63.6 11.5 %copy-start.5 = (f32[384,512]{1,0:T(8,128)S(1)}, f32[384,512]{1,0:T(8,128)}, u32[]{:S(2)}) copy-start(f32[384,512]{1,0:T(8,128)} %get-tuple-element.59) | copy-start | bytes 2359300
  74.6 2.6 %collective-permute-start.14 = (f32[384,640]{1,0:T(8,128)S(1)}, f32[384,640]{1,0:T(8,128)S(1)}, u32[]{:S(2)}, u32[]{:S(2)}) collective-permute-start(f32[384,640]{1,0:T(8,128)S(1)} %slice.8.refs_4_), channel_id=1, source_target_pairs={{0,1},{1,0},{2,3},{3,2},{4,5},{5,4},{6,7},{7,6},{8,9},{9,8},{10,11... | collective-permute-start | bytes 2949128 | tf_op jit(solution)/shard_map/ppermute | solution.py:27
  74.6 4.0 %collective-permute-start.15 = (f32[384,640]{1,0:T(8,128)S(1)}, f32[384,640]{1,0:T(8,128)S(1)}, u32[]{:S(2)}, u32[]{:S(2)}) collective-permute-start(f32[384,640]{1,0:T(8,128)S(1)} %collective-permute-done.12.refs_5_), channel_id=1, source_target_pairs={{0,1},{1,0},{2,3},{3,2},{4,5},{5,4},{6,7},{7,6},{8,9},{9,8},{10,11... | collective-permute-start | bytes 2949128 | tf_op jit(solution)/shard_map/ppermute | solution.py:27
  75.1 20.8 %collective-permute-start.16 = (f32[384,512]{1,0:T(8,128)S(1)}, f32[384,512]{1,0:T(8,128)S(1)}, u32[]{:S(2)}, u32[]{:S(2)}) collective-permute-start(f32[384,512]{1,0:T(8,128)S(1)} %copy-done.5), channel_id=1, source_target_pairs={{0,4},{4,0},{8,12},{12,8},{16,20},{20,16},{24,28},{28,24},{1,5},{5... | collective-permute-start | bytes 2359304 | tf_op jit(solution)/shard_map/ppermute | solution.py:32

commit v3 on v2

--- a/solution.py
+++ b/solution.py
@@ -544,7 +544,7 @@
     )(matrix, weights[None])
     far_slab = from_sibling(slab)
     slabs = spread([slab])
-    cuts = (0, 3, 5, 7, len(rest))
+    cuts = (0, 2, 7, len(rest))
     rest = [rest[low:high] for low, high in zip(cuts, cuts[1:])]
     chosen = corner + [1]
     wanted = [chosen, chosen + rest[0], *rest[1:]]
@@ -613,8 +613,8 @@
         compiler_params=large,
         cost_estimate=pl.CostEstimate(flops=2 * 10**9, bytes_accessed=2**22, transcendentals=0),
         name="own",
-    )(table, heads, weights[None], kept, after(inverse, far[1]), matrix, *near_edges, *other_edges)
-    other_far_edges = [from_front(after(piece, column, far[2]), 1) for piece in far_edges]
+    )(table, heads, weights[None], kept, inverse, matrix, *near_edges, *other_edges)
+    other_far_edges = [from_front(after(piece, column, far[1]), 1) for piece in far_edges]
     parent_panel, update = pl.pallas_call(
         functools.partial(parent_kernel, width=width, **sizes),
         out_shape=(jax.ShapeDtypeStruct((rows, TILE), f32), update_shape),

time: 100 us -> 99.5 us (level)
    ppermute x5 -> x4, starting transfers between devices: 6.24 us -> 5.75 us  [from_sibling(): return lax.ppermute(value, 'leaf', pairs)]
    ppermute x5 -> x4, waiting for transfers between devices: 8.29 us -> 7.81 us  [from_sibling(): return lax.ppermute(value, 'leaf', pairs)]
  transfers between devices with their start and end apart: 17 -> 16, of which waited for: 10 -> 10; matrix products, arithmetic and copies ran while one was open for 0% -> 0% of each run, Pallas kernels for 59% -> 60%
where the time goes in v3:
time: 99.5 us; the launch traced here: 99.4 us
  Pallas kernels  65.6 us (66%)
  waiting for transfers between devices  20.2 us (20%)
  starting transfers between devices  12.5 us (13%)
    pallas_call x1, Pallas kernels, one_front(): pl.pallas_call(functools.partial(half_kernel, first=0, last=middle), out_...  20.2 us
    pallas_call x1, Pallas kernels, one_front(): pl.pallas_call(functools.partial(parent_kernel, width=width, **sizes), ou...  17.3 us
    ppermute x12, waiting for transfers between devices, from_front(): return lax.ppermute(value, 'front', pairs)  12.4 us
    pallas_call x1, Pallas kernels, one_front(): pl.pallas_call(functools.partial(own_kernel, width=width, **sizes), out_s...  11 us
    ppermute x4, waiting for transfers between devices, from_sibling(): return lax.ppermute(value, 'leaf', pairs)  7.81 us
    ppermute x12, starting transfers between devices, from_front(): return lax.ppermute(value, 'front', pairs)  6.74 us
    pallas_call x1, Pallas kernels, one_front(): pl.pallas_call(functools.partial(half_kernel, first=middle, last=separato...  5.88 us
    ppermute x4, starting transfers between devices, from_sibling(): return lax.ppermute(value, 'leaf', pairs)  5.75 us
  transfers between devices with their start and end apart: 16, of which 10 were waited for; matrix products, arithmetic and copies ran while one was open for 0% of the time, Pallas kernels for 60%

profile of v3, /device:TPU:0, one launch (start us, length us, event | category | flops | bytes accessed | tf_op | source)
XLA Modules:
  0.0 99.4 jit_solution(14079248456174872417)
XLA Ops:
  0.6 2.5 %slab.1 = (f32[136,512]{1,0:T(8,128)}, f32[136,512]{1,0:T(8,128)}) custom-call(f32[512,2048]{1,0:T(8,128)} %bitcast.6, f32[1,512]{1,0:T(1,128)} %bitcast.12), custom_call_target="tpu_custom_call" | custom-call | bytes 524288 | tf_op jit(solution)/shard_map/slab/pallas_call | solution.py:535
  3.1 3.0 %collective-permute-start.3 = (f32[136,512]{1,0:T(8,128)}, f32[136,512]{1,0:T(8,128)S(1)}, u32[]{:S(2)}, u32[]{:S(2)}) collective-permute-start(f32[136,512]{1,0:T(8,128)} %get-tuple-element.30), channel_id=1, source_target_pairs={{0,4},{4,0},{8,12},{12,8},{16,20},{20,16},{24,28},{28,24},{1,5},{5... | collective-permute-start | bytes 835592 | tf_op jit(solution)/shard_map/ppermute | solution.py:32
  6.2 1.5 %collective-permute-start = (f32[136,512]{1,0:T(8,128)}, f32[136,512]{1,0:T(8,128)S(1)}, u32[]{:S(2)}, u32[]{:S(2)}) collective-permute-start(f32[136,512]{1,0:T(8,128)} %get-tuple-element.30), channel_id=1, source_target_pairs={{0,2},{1,3},{2,0},{3,1},{4,6},{5,7},{6,4},{7,5},{8,10},{9,11},{10,... | collective-permute-start | bytes 835592 | tf_op jit(solution)/shard_map/ppermute | solution.py:27
  7.7 4.9 %body.1 = (f32[384,640]{1,0:T(8,128)}, f32[384,896]{1,0:T(8,128)}, f32[384,640]{1,0:T(8,128)}, f32[384,512]{1,0:T(8,128)}) custom-call(f32[512,2048]{1,0:T(8,128)} %bitcast.7), custom_call_target="tpu_custom_call" | custom-call | bytes 8388608 | tf_op jit(solution)/shard_map/body/pallas_call | solution.py:551
  12.5 0.5 collective-permute-done.3.refs_4_
  13.0 1.5 %collective-permute-done.refs_1_ = f32[136,512]{1,0:T(8,128)S(1)} collective-permute-done((f32[136,512]{1,0:T(8,128)}, f32[136,512]{1,0:T(8,128)S(1)}, u32[]{:S(2)}, u32[]{:S(2)}) %collective-permute-start) | collective-permute-done | bytes 278560 | tf_op jit(solution)/shard_map/ppermute | solution.py:27
  14.5 1.5 %collective-permute-start.4 = (f32[136,512]{1,0:T(8,128)S(1)}, f32[136,512]{1,0:T(8,128)S(1)}, u32[]{:S(2)}, u32[]{:S(2)}) collective-permute-start(f32[136,512]{1,0:T(8,128)S(1)} %collective-permute-done.3.refs_4_), channel_id=1, source_target_pairs={{0,2},{1,3},{2,0},{3,1},{4,6},{5,7},{6,4},{7,5},{8,10},{9,11},{10,... | collective-permute-start | bytes 835592 | tf_op jit(solution)/shard_map/ppermute | solution.py:27
  16.0 5.7 %collective-permute-done.4.refs_5_ = f32[136,512]{1,0:T(8,128)S(1)} collective-permute-done((f32[136,512]{1,0:T(8,128)S(1)}, f32[136,512]{1,0:T(8,128)S(1)}, u32[]{:S(2)}, u32[]{:S(2)}) %collective-permute-start.4) | collective-permute-done | bytes 278560 | tf_op jit(solution)/shard_map/ppermute | solution.py:27
  21.7 1.5 %collective-permute-start.9 = (f32[384,640]{1,0:T(8,128)}, f32[384,640]{1,0:T(8,128)S(1)}, u32[]{:S(2)}, u32[]{:S(2)}) collective-permute-start(f32[384,640]{1,0:T(8,128)} %get-tuple-element.39.refs_6_), channel_id=1, source_target_pairs={{0,2},{1,3},{2,0},{3,1},{4,6},{5,7},{6,4},{7,5},{8,10},{9,11},{10,... | collective-permute-start | bytes 2949128 | tf_op jit(solution)/shard_map/ppermute | solution.py:27
  23.2 0.6 collective-permute-start.7
  23.8 0.5 collective-permute-start.5
  24.3 1.0 %collective-permute-done.1.refs_2_ = f32[136,512]{1,0:T(8,128)S(1)} collective-permute-done((f32[136,512]{1,0:T(8,128)S(1)}, f32[136,512]{1,0:T(8,128)S(1)}, u32[]{:S(2)}, u32[]{:S(2)}) %collective-permute-start.1) | collective-permute-done | bytes 278560 | tf_op jit(solution)/shard_map/ppermute | solution.py:27
  25.4 0.1 collective-permute-start.6
  25.5 0.7 collective-permute-done.2.refs_3_
  26.2 0.8 collective-permute-done.6.refs_7_
  26.9 20.2 %corner_first.1 = (f32[2,512,512]{2,1,0:T(8,128)S(1)}, f32[2,512,512]{2,1,0:T(8,128)S(1)}, f32[2,8,512]{2,1,0:T(8,128)S(1)}) custom-call(f32[136,512]{1,0:T(8,128)S(1)} %copy-done.2, f32[136,512]{1,0:T(8,128)S(1)} %collective-permute-done.refs_1_, f32[136,512]{1,0:T(8,128)S(1)} %collective-permute-done.1.refs_2_, ...), custom_call_target="tpu_custom_call" | custom-call | flops 3000000000 | bytes 4194304 | tf_op jit(solution)/shard_map/corner_first/pallas_call | solution.py:573
  47.2 0.2 collective-permute-start.8
  47.4 0.4 collective-permute-start.10
  47.7 1.4 %collective-permute-start.12 = (f32[384,640]{1,0:T(8,128)S(1)}, f32[384,640]{1,0:T(8,128)S(1)}, u32[]{:S(2)}, u32[]{:S(2)}) collective-permute-start(f32[384,640]{1,0:T(8,128)S(1)} %copy-done.5), channel_id=1, source_target_pairs={{0,4},{4,0},{8,12},{12,8},{16,20},{20,16},{24,28},{28,24},{1,5},{5... | collective-permute-start | bytes 2949128 | tf_op jit(solution)/shard_map/ppermute | solution.py:32
  49.2 6.2 %collective-permute-done.7 = f32[384,896]{1,0:T(8,128)S(1)} collective-permute-done((f32[384,896]{1,0:T(8,128)}, f32[384,896]{1,0:T(8,128)S(1)}, u32[]{:S(2)}, u32[]{:S(2)}) %collective-permute-start.7) | collective-permute-done | bytes 1376288 | tf_op jit(solution)/shard_map/ppermute | solution.py:32
  55.3 0.1 slice.8.refs_4_
  55.4 0.5 collective-permute-start.11
  55.9 0.0 copy-start.3
  56.0 5.9 %corner_second.1.refs_4_.refs_1_ = f32[2,512,512]{2,1,0:T(8,128)S(1)} custom-call(f32[2,512,512]{2,1,0:T(8,128)S(1)} %get-tuple-element.41.refs_0_, f32[2,512,512]{2,1,0:T(8,128)S(1)} %get-tuple-element.42.refs_1_), custom_call_target="tpu_custom_call" | custom-call | flops 3000000000 | bytes 4194304 | tf_op jit(solution)/shard_map/corner_second/pallas_call | solution.py:588
  61.9 11.0 %own.1 = (f32[512,512]{1,0:T(8,128)}, f32[4096,128]{1,0:T(8,128)S(1)}, f32[640,4096]{1,0:T(8,128)S(1)}) custom-call(s32[8,12]{1,0:T(8,128)S(1)} %bitcast.9, f32[2,8,512]{2,1,0:T(8,128)S(1)} %get-tuple-element.34.refs_1_, f32[1,512]{1,0:T(1,128)S(1)} %bitcast.13, f32[136,512]{1,0:T(8,128)S(1)} %copy-done.2, f32[2,512,512]{2,1,0:T(8,128)S(1)} %corner_second.1.refs_4_.refs_1_, ...), custom_call_target="tpu_custom_call" | custom-call | flops 2000000000 | bytes 4194304 | tf_op jit(solution)/shard_map/own/pallas_call | solution.py:603
  72.9 1.1 %collective-permute-done.12.refs_1_ = f32[384,640]{1,0:T(8,128)S(1)} collective-permute-done((f32[384,640]{1,0:T(8,128)S(1)}, f32[384,640]{1,0:T(8,128)S(1)}, u32[]{:S(2)}, u32[]{:S(2)}) %collective-permute-start.12) | collective-permute-done | bytes 983072 | tf_op jit(solution)/shard_map/ppermute | solution.py:32
  74.0 0.5 collective-permute-start.14
  74.5 0.7 collective-permute-start.15
  75.2 1.3 %collective-permute-done.13.refs_6_ = f32[384,640]{1,0:T(8,128)S(1)} collective-permute-done((f32[384,640]{1,0:T(8,128)S(1)}, f32[384,640]{1,0:T(8,128)S(1)}, u32[]{:S(2)}, u32[]{:S(2)}) %collective-permute-start.13) | collective-permute-done | bytes 983072 | tf_op jit(solution)/shard_map/ppermute | solution.py:27
  76.6 1.4 %collective-permute-done.14.refs_7_ = f32[384,640]{1,0:T(8,128)S(1)} collective-permute-done((f32[384,640]{1,0:T(8,128)S(1)}, f32[384,640]{1,0:T(8,128)S(1)}, u32[]{:S(2)}, u32[]{:S(2)}) %collective-permute-start.14) | collective-permute-done | bytes 983072 | tf_op jit(solution)/shard_map/ppermute | solution.py:27
  78.0 17.3 %parent.1 = (f32[512,128]{1,0:T(8,128)}, f32[512,3968]{1,0:T(8,128)}) custom-call(s32[8,12]{1,0:T(8,128)S(1)} %bitcast.10, f32[2,512,512]{2,1,0:T(8,128)S(1)} %corner_second.1.refs_4_.refs_1_, f32[4096,128]{1,0:T(8,128)S(1)} %get-tuple-element.44.refs_2_, f32[640,4096]{1,0:T(8,128)S(1)} %get-tuple-element.45.refs_3_, f32[384,640]{1,0:T(8,128)S(1)} %slice.8.refs_4_, ...), custom_call_target="tpu_custom_call" | custom-call | flops 2000000000 | bytes 4194304 | tf_op jit(solution)/shard_map/parent/pallas_call | solution.py:618
  95.3 3.9 %far.1 = f32[512,3968]{1,0:T(8,128)} custom-call(s32[8,12]{1,0:T(8,128)S(1)} %bitcast.11, f32[384,256]{1,0:T(8,128)S(1)} %slice.9.refs_0_, f32[384,640]{1,0:T(8,128)S(1)} %collective-permute-done.12.refs_1_, f32[384,512]{1,0:T(8,128)S(1)} %collective-permute-done.15.refs_2_, f32[512,3968]{1,0:T(8,128)} %get-tuple-element.54.refs_3_), custom_call_target="tpu_custom_call", output_to_operand_aliasing={{}: (4, {})} | custom-call | flops 2000000000 | bytes 4194304 | tf_op jit(solution)/shard_map/far/pallas_call | solution.py:637
  (25 shorter events, 0.1 us)
Async XLA Ops:
  3.1 20.7 %copy-start.7 = (f32[136,512]{1,0:T(8,128)S(1)}, f32[136,512]{1,0:T(8,128)}, u32[]{:S(2)}) copy-start(f32[136,512]{1,0:T(8,128)} %get-tuple-element.30) | copy-start | bytes 835588
  3.1 23.8 %copy-start.2 = (f32[136,512]{1,0:T(8,128)S(1)}, f32[136,512]{1,0:T(8,128)}, u32[]{:S(2)}) copy-start(f32[136,512]{1,0:T(8,128)} %get-tuple-element.29.refs_0_.refs_3_) | copy-start | bytes 835588
  3.1 9.9 %collective-permute-start.3 = (f32[136,512]{1,0:T(8,128)}, f32[136,512]{1,0:T(8,128)S(1)}, u32[]{:S(2)}, u32[]{:S(2)}) collective-permute-start(f32[136,512]{1,0:T(8,128)} %get-tuple-element.30), channel_id=1, source_target_pairs={{0,4},{4,0},{8,12},{12,8},{16,20},{20,16},{24,28},{28,24},{1,5},{5... | collective-permute-start | bytes 835592 | tf_op jit(solution)/shard_map/ppermute | solution.py:32
  6.2 8.3 %collective-permute-start = (f32[136,512]{1,0:T(8,128)}, f32[136,512]{1,0:T(8,128)S(1)}, u32[]{:S(2)}, u32[]{:S(2)}) collective-permute-start(f32[136,512]{1,0:T(8,128)} %get-tuple-element.30), channel_id=1, source_target_pairs={{0,2},{1,3},{2,0},{3,1},{4,6},{5,7},{6,4},{7,5},{8,10},{9,11},{10,... | collective-permute-start | bytes 835592 | tf_op jit(solution)/shard_map/ppermute | solution.py:27
  14.5 7.2 %collective-permute-start.4 = (f32[136,512]{1,0:T(8,128)S(1)}, f32[136,512]{1,0:T(8,128)S(1)}, u32[]{:S(2)}, u32[]{:S(2)}) collective-permute-start(f32[136,512]{1,0:T(8,128)S(1)} %collective-permute-done.3.refs_4_), channel_id=1, source_target_pairs={{0,2},{1,3},{2,0},{3,1},{4,6},{5,7},{6,4},{7,5},{8,10},{9,11},{10,... | collective-permute-start | bytes 835592 | tf_op jit(solution)/shard_map/ppermute | solution.py:27
  21.7 25.7 %collective-permute-start.9 = (f32[384,640]{1,0:T(8,128)}, f32[384,640]{1,0:T(8,128)S(1)}, u32[]{:S(2)}, u32[]{:S(2)}) collective-permute-start(f32[384,640]{1,0:T(8,128)} %get-tuple-element.39.refs_6_), channel_id=1, source_target_pairs={{0,2},{1,3},{2,0},{3,1},{4,6},{5,7},{6,4},{7,5},{8,10},{9,11},{10,... | collective-permute-start | bytes 2949128 | tf_op jit(solution)/shard_map/ppermute | solution.py:27
  23.2 32.1 %collective-permute-start.7 = (f32[384,896]{1,0:T(8,128)}, f32[384,896]{1,0:T(8,128)S(1)}, u32[]{:S(2)}, u32[]{:S(2)}) collective-permute-start(f32[384,896]{1,0:T(8,128)} %get-tuple-element.37), channel_id=1, source_target_pairs={{0,4},{4,0},{8,12},{12,8},{16,20},{20,16},{24,28},{28,24},{1,5},{5... | collective-permute-start | bytes 4128776 | tf_op jit(solution)/shard_map/ppermute | solution.py:32
  23.8 1.6 %collective-permute-start.1 = (f32[136,512]{1,0:T(8,128)S(1)}, f32[136,512]{1,0:T(8,128)S(1)}, u32[]{:S(2)}, u32[]{:S(2)}) collective-permute-start(f32[136,512]{1,0:T(8,128)S(1)} %copy-done.7), channel_id=1, source_target_pairs={{0,1},{1,0},{2,3},{3,2},{4,5},{5,4},{6,7},{7,6},{8,9},{9,8},{10,11... | collective-permute-start | bytes 835592 | tf_op jit(solution)/shard_map/ppermute | solution.py:27
  23.8 2.4 %collective-permute-start.5 = (f32[136,512]{1,0:T(8,128)S(1)}, f32[136,512]{1,0:T(8,128)S(1)}, u32[]{:S(2)}, u32[]{:S(2)}) collective-permute-start(f32[136,512]{1,0:T(8,128)S(1)} %collective-permute-done.3.refs_4_), channel_id=1, source_target_pairs={{0,1},{1,0},{2,3},{3,2},{4,5},{5,4},{6,7},{7,6},{8,9},{9,8},{10,11... | collective-permute-start | bytes 835592 | tf_op jit(solution)/shard_map/ppermute | solution.py:27
  24.3 1.8 %collective-permute-start.2 = (f32[136,512]{1,0:T(8,128)S(1)}, f32[136,512]{1,0:T(8,128)S(1)}, u32[]{:S(2)}, u32[]{:S(2)}) collective-permute-start(f32[136,512]{1,0:T(8,128)S(1)} %collective-permute-done.refs_1_), channel_id=1, source_target_pairs={{0,1},{1,0},{2,3},{3,2},{4,5},{5,4},{6,7},{7,6},{8,9},{9,8},{10,11... | collective-permute-start | bytes 835592 | tf_op jit(solution)/shard_map/ppermute | solution.py:27
  25.4 1.6 %collective-permute-start.6 = (f32[136,512]{1,0:T(8,128)S(1)}, f32[136,512]{1,0:T(8,128)S(1)}, u32[]{:S(2)}, u32[]{:S(2)}) collective-permute-start(f32[136,512]{1,0:T(8,128)S(1)} %collective-permute-done.4.refs_5_), channel_id=1, source_target_pairs={{0,1},{1,0},{2,3},{3,2},{4,5},{5,4},{6,7},{7,6},{8,9},{9,8},{10,11... | collective-permute-start | bytes 835592 | tf_op jit(solution)/shard_map/ppermute | solution.py:27
  26.9 20.2 %copy-start.1 = (f32[384,640]{1,0:T(8,128)S(1)}, f32[384,640]{1,0:T(8,128)}, u32[]{:S(2)}) copy-start(f32[384,640]{1,0:T(8,128)} %get-tuple-element.39.refs_6_) | copy-start | bytes 2949124
  26.9 20.8 %copy-start.5 = (f32[384,640]{1,0:T(8,128)S(1)}, f32[384,640]{1,0:T(8,128)}, u32[]{:S(2)}) copy-start(f32[384,640]{1,0:T(8,128)} %get-tuple-element.48) | copy-start | bytes 2949124
  47.2 8.8 %collective-permute-start.8 = (f32[384,640]{1,0:T(8,128)S(1)}, f32[384,640]{1,0:T(8,128)S(1)}, u32[]{:S(2)}, u32[]{:S(2)}) collective-permute-start(f32[384,640]{1,0:T(8,128)S(1)} %copy-done.1), channel_id=1, source_target_pairs={{0,1},{1,0},{2,3},{3,2},{4,5},{5,4},{6,7},{7,6},{8,9},{9,8},{10,11... | collective-permute-start | bytes 2949128 | tf_op jit(solution)/shard_map/ppermute | solution.py:27
  47.4 8.6 %collective-permute-start.10 = (f32[384,640]{1,0:T(8,128)S(1)}, f32[384,640]{1,0:T(8,128)S(1)}, u32[]{:S(2)}, u32[]{:S(2)}) collective-permute-start(f32[384,640]{1,0:T(8,128)S(1)} %collective-permute-done.9.refs_7_), channel_id=1, source_target_pairs={{0,1},{1,0},{2,3},{3,2},{4,5},{5,4},{6,7},{7,6},{8,9},{9,8},{10,11... | collective-permute-start | bytes 2949128 | tf_op jit(solution)/shard_map/ppermute | solution.py:27
  47.7 26.3 %collective-permute-start.12 = (f32[384,640]{1,0:T(8,128)S(1)}, f32[384,640]{1,0:T(8,128)S(1)}, u32[]{:S(2)}, u32[]{:S(2)}) collective-permute-start(f32[384,640]{1,0:T(8,128)S(1)} %copy-done.5), channel_id=1, source_target_pairs={{0,4},{4,0},{8,12},{12,8},{16,20},{20,16},{24,28},{28,24},{1,5},{5... | collective-permute-start | bytes 2949128 | tf_op jit(solution)/shard_map/ppermute | solution.py:32
  55.4 18.6 %collective-permute-start.11 = (f32[384,640]{1,0:T(8,128)S(1)}, f32[384,640]{1,0:T(8,128)S(1)}, u32[]{:S(2)}, u32[]{:S(2)}) collective-permute-start(f32[384,640]{1,0:T(8,128)S(1)} %slice.8.refs_4_), channel_id=1, source_target_pairs={{0,2},{1,3},{2,0},{3,1},{4,6},{5,7},{6,4},{7,5},{8,10},{9,11},{10,... | collective-permute-start | bytes 2949128 | tf_op jit(solution)/shard_map/ppermute | solution.py:27
  55.9 5.9 %copy-start = (f32[1,1,512,2048]{3,2,1,0:T(8,128)S(1)}, f32[1,1,512,2048]{3,2,1,0:T(8,128)}, u32[]{:S(2)}) copy-start(f32[1,1,512,2048]{3,2,1,0:T(8,128)} %param.3) | copy-start | bytes 12582916
  55.9 5.9 %copy-start.3 = (s32[8,1,12]{2,1,0:T(1,128)S(1)}, s32[8,1,12]{2,1,0:T(1,128)}, u32[]{:S(2)}) copy-start(s32[8,1,12]{2,1,0:T(1,128)} %param.5) | copy-start | bytes 1156
  56.0 5.9 %copy-start.4 = (f32[1,1,512]{2,1,0:T(1,128)S(1)}, f32[1,1,512]{2,1,0:T(1,128)}, u32[]{:S(2)}) copy-start(f32[1,1,512]{2,1,0:T(1,128)} %param.4) | copy-start | bytes 6148
  61.9 12.6 %copy-start.6 = (f32[384,512]{1,0:T(8,128)S(1)}, f32[384,512]{1,0:T(8,128)}, u32[]{:S(2)}) copy-start(f32[384,512]{1,0:T(8,128)} %get-tuple-element.53) | copy-start | bytes 2359300
  74.0 2.6 %collective-permute-start.13 = (f32[384,640]{1,0:T(8,128)S(1)}, f32[384,640]{1,0:T(8,128)S(1)}, u32[]{:S(2)}, u32[]{:S(2)}) collective-permute-start(f32[384,640]{1,0:T(8,128)S(1)} %slice.8.refs_4_), channel_id=1, source_target_pairs={{0,1},{1,0},{2,3},{3,2},{4,5},{5,4},{6,7},{7,6},{8,9},{9,8},{10,11... | collective-permute-start | bytes 2949128 | tf_op jit(solution)/shard_map/ppermute | solution.py:27
  74.0 4.0 %collective-permute-start.14 = (f32[384,640]{1,0:T(8,128)S(1)}, f32[384,640]{1,0:T(8,128)S(1)}, u32[]{:S(2)}, u32[]{:S(2)}) collective-permute-start(f32[384,640]{1,0:T(8,128)S(1)} %collective-permute-done.11.refs_5_), channel_id=1, source_target_pairs={{0,1},{1,0},{2,3},{3,2},{4,5},{5,4},{6,7},{7,6},{8,9},{9,8},{10,11... | collective-permute-start | bytes 2949128 | tf_op jit(solution)/shard_map/ppermute | solution.py:27
  74.5 20.8 %collective-permute-start.15 = (f32[384,512]{1,0:T(8,128)S(1)}, f32[384,512]{1,0:T(8,128)S(1)}, u32[]{:S(2)}, u32[]{:S(2)}) collective-permute-start(f32[384,512]{1,0:T(8,128)S(1)} %copy-done.6), channel_id=1, source_target_pairs={{0,4},{4,0},{8,12},{12,8},{16,20},{20,16},{24,28},{28,24},{1,5},{5... | collective-permute-start | bytes 2359304 | tf_op jit(solution)/shard_map/ppermute | solution.py:32

commit v4 on v3

--- a/solution.py
+++ b/solution.py
@@ -544,7 +544,7 @@
     )(matrix, weights[None])
     far_slab = from_sibling(slab)
     slabs = spread([slab])
-    cuts = (0, 2, 7, len(rest))
+    cuts = (0, 3, 7, len(rest))
     rest = [rest[low:high] for low, high in zip(cuts, cuts[1:])]
     chosen = corner + [1]
     wanted = [chosen, chosen + rest[0], *rest[1:]]

time: 99.5 us -> 96.7 us (0.972)
  waiting for transfers between devices: 20.2 us -> 18.2 us
  starting transfers between devices: 12.5 us -> 11.2 us
    ppermute x4, waiting for transfers between devices: 7.81 us -> 4.3 us  [from_sibling(): return lax.ppermute(value, 'leaf', pairs)]
    ppermute x12, waiting for transfers between devices: 12.4 us -> 13.9 us  [from_front(): return lax.ppermute(value, 'front', pairs)]
  transfers between devices with their start and end apart: 16 -> 16, of which waited for: 10 -> 10; matrix products, arithmetic and copies ran while one was open for 0% -> 0% of each run, Pallas kernels for 60% -> 62%
where the time goes in v4:
time: 96.7 us; the launch traced here: 96.2 us
  Pallas kernels  65.7 us (68%)
  waiting for transfers between devices  18.2 us (19%)
  starting transfers between devices  11.2 us (12%)
  between operations  0.97 us (1%)
    pallas_call x1, Pallas kernels, one_front(): pl.pallas_call(functools.partial(half_kernel, first=0, last=middle), out_...  20.2 us
    pallas_call x1, Pallas kernels, one_front(): pl.pallas_call(functools.partial(parent_kernel, width=width, **sizes), ou...  17.3 us
    ppermute x12, waiting for transfers between devices, from_front(): return lax.ppermute(value, 'front', pairs)  13.9 us
    pallas_call x1, Pallas kernels, one_front(): pl.pallas_call(functools.partial(own_kernel, width=width, **sizes), out_s...  11 us
    ppermute x12, starting transfers between devices, from_front(): return lax.ppermute(value, 'front', pairs)  6.3 us
    pallas_call x1, Pallas kernels, one_front(): pl.pallas_call(functools.partial(half_kernel, first=middle, last=separato...  5.88 us
    ppermute x4, starting transfers between devices, from_sibling(): return lax.ppermute(value, 'leaf', pairs)  4.91 us
    pallas_call x1, Pallas kernels, one_front(): pl.pallas_call(functools.partial(body_kernel, skip=skip, wanted=wanted),...  4.88 us
  transfers between devices with their start and end apart: 16, of which 10 were waited for; matrix products, arithmetic and copies ran while one was open for 0% of the time, Pallas kernels for 62%

profile of v4, /device:TPU:0, one launch (start us, length us, event | category | flops | bytes accessed | tf_op | source)
XLA Modules:
  0.0 96.2 jit_solution(8244425218981998234)
XLA Ops:
  0.6 2.5 %slab.1 = (f32[136,512]{1,0:T(8,128)}, f32[136,512]{1,0:T(8,128)}) custom-call(f32[512,2048]{1,0:T(8,128)} %bitcast.6, f32[1,512]{1,0:T(1,128)} %bitcast.12), custom_call_target="tpu_custom_call" | custom-call | bytes 524288 | tf_op jit(solution)/shard_map/slab/pallas_call | solution.py:535
  3.1 3.0 %collective-permute-start.3 = (f32[136,512]{1,0:T(8,128)}, f32[136,512]{1,0:T(8,128)S(1)}, u32[]{:S(2)}, u32[]{:S(2)}) collective-permute-start(f32[136,512]{1,0:T(8,128)} %get-tuple-element.30), channel_id=1, source_target_pairs={{0,4},{4,0},{8,12},{12,8},{16,20},{20,16},{24,28},{28,24},{1,5},{5... | collective-permute-start | bytes 835592 | tf_op jit(solution)/shard_map/ppermute | solution.py:32
  6.2 1.5 %collective-permute-start = (f32[136,512]{1,0:T(8,128)}, f32[136,512]{1,0:T(8,128)S(1)}, u32[]{:S(2)}, u32[]{:S(2)}) collective-permute-start(f32[136,512]{1,0:T(8,128)} %get-tuple-element.30), channel_id=1, source_target_pairs={{0,2},{1,3},{2,0},{3,1},{4,6},{5,7},{6,4},{7,5},{8,10},{9,11},{10,... | collective-permute-start | bytes 835592 | tf_op jit(solution)/shard_map/ppermute | solution.py:27
  7.6 4.9 %body.1 = (f32[384,640]{1,0:T(8,128)}, f32[384,1024]{1,0:T(8,128)}, f32[384,512]{1,0:T(8,128)}, f32[384,512]{1,0:T(8,128)}) custom-call(f32[512,2048]{1,0:T(8,128)} %bitcast.7), custom_call_target="tpu_custom_call" | custom-call | bytes 8388608 | tf_op jit(solution)/shard_map/body/pallas_call | solution.py:551
  12.5 0.5 collective-permute-done.3.refs_4_
  13.0 1.5 %collective-permute-done.refs_1_ = f32[136,512]{1,0:T(8,128)S(1)} collective-permute-done((f32[136,512]{1,0:T(8,128)}, f32[136,512]{1,0:T(8,128)S(1)}, u32[]{:S(2)}, u32[]{:S(2)}) %collective-permute-start) | collective-permute-done | bytes 278560 | tf_op jit(solution)/shard_map/ppermute | solution.py:27
  14.5 1.5 %collective-permute-start.4 = (f32[136,512]{1,0:T(8,128)S(1)}, f32[136,512]{1,0:T(8,128)S(1)}, u32[]{:S(2)}, u32[]{:S(2)}) collective-permute-start(f32[136,512]{1,0:T(8,128)S(1)} %collective-permute-done.3.refs_4_), channel_id=1, source_target_pairs={{0,2},{1,3},{2,0},{3,1},{4,6},{5,7},{6,4},{7,5},{8,10},{9,11},{10,... | collective-permute-start | bytes 835592 | tf_op jit(solution)/shard_map/ppermute | solution.py:27
  16.0 0.5 collective-permute-start.7
  16.5 5.2 %collective-permute-done.4.refs_5_ = f32[136,512]{1,0:T(8,128)S(1)} collective-permute-done((f32[136,512]{1,0:T(8,128)S(1)}, f32[136,512]{1,0:T(8,128)S(1)}, u32[]{:S(2)}, u32[]{:S(2)}) %collective-permute-start.4) | collective-permute-done | bytes 278560 | tf_op jit(solution)/shard_map/ppermute | solution.py:27
  21.7 1.5 %collective-permute-start.9 = (f32[384,640]{1,0:T(8,128)}, f32[384,640]{1,0:T(8,128)S(1)}, u32[]{:S(2)}, u32[]{:S(2)}) collective-permute-start(f32[384,640]{1,0:T(8,128)} %get-tuple-element.39.refs_6_), channel_id=1, source_target_pairs={{0,2},{1,3},{2,0},{3,1},{4,6},{5,7},{6,4},{7,5},{8,10},{9,11},{10,... | collective-permute-start | bytes 2949128 | tf_op jit(solution)/shard_map/ppermute | solution.py:27
  23.2 0.5 collective-permute-start.5
  23.7 1.0 %collective-permute-done.1.refs_2_ = f32[136,512]{1,0:T(8,128)S(1)} collective-permute-done((f32[136,512]{1,0:T(8,128)S(1)}, f32[136,512]{1,0:T(8,128)S(1)}, u32[]{:S(2)}, u32[]{:S(2)}) %collective-permute-start.1) | collective-permute-done | bytes 278560 | tf_op jit(solution)/shard_map/ppermute | solution.py:27
  24.7 0.1 collective-permute-start.6
  24.9 0.7 collective-permute-done.2.refs_3_
  25.5 0.8 collective-permute-done.6.refs_7_
  26.3 20.2 %corner_first.1 = (f32[2,512,512]{2,1,0:T(8,128)S(1)}, f32[2,512,512]{2,1,0:T(8,128)S(1)}, f32[2,8,512]{2,1,0:T(8,128)S(1)}) custom-call(f32[136,512]{1,0:T(8,128)S(1)} %copy-done.2, f32[136,512]{1,0:T(8,128)S(1)} %collective-permute-done.refs_1_, f32[136,512]{1,0:T(8,128)S(1)} %collective-permute-done.1.refs_2_, ...), custom_call_target="tpu_custom_call" | custom-call | flops 3000000000 | bytes 4194304 | tf_op jit(solution)/shard_map/corner_first/pallas_call | solution.py:573
  46.5 0.2 collective-permute-start.8
  46.7 0.4 collective-permute-start.10
  47.1 3.7 %collective-permute-done.7 = f32[384,1024]{1,0:T(8,128)S(1)} collective-permute-done((f32[384,1024]{1,0:T(8,128)}, f32[384,1024]{1,0:T(8,128)S(1)}, u32[]{:S(2)}, u32[]{:S(2)}) %collective-permute-start.7) | collective-permute-done | bytes 1572896 | tf_op jit(solution)/shard_map/ppermute | solution.py:32
  50.8 0.1 slice.8.refs_4_
  50.9 0.6 collective-permute-start.11
  51.5 0.7 collective-permute-start.12
  52.2 0.0 copy-start.3
  52.2 5.9 %corner_second.1.refs_4_.refs_1_ = f32[2,512,512]{2,1,0:T(8,128)S(1)} custom-call(f32[2,512,512]{2,1,0:T(8,128)S(1)} %get-tuple-element.41.refs_0_, f32[2,512,512]{2,1,0:T(8,128)S(1)} %get-tuple-element.42.refs_1_), custom_call_target="tpu_custom_call" | custom-call | flops 3000000000 | bytes 4194304 | tf_op jit(solution)/shard_map/corner_second/pallas_call | solution.py:588
  58.2 11.0 %own.1 = (f32[512,512]{1,0:T(8,128)}, f32[4096,128]{1,0:T(8,128)S(1)}, f32[640,4096]{1,0:T(8,128)S(1)}) custom-call(s32[8,12]{1,0:T(8,128)S(1)} %bitcast.9, f32[2,8,512]{2,1,0:T(8,128)S(1)} %get-tuple-element.34.refs_1_, f32[1,512]{1,0:T(1,128)S(1)} %bitcast.13, f32[136,512]{1,0:T(8,128)S(1)} %copy-done.2, f32[2,512,512]{2,1,0:T(8,128)S(1)} %corner_second.1.refs_4_.refs_1_, ...), custom_call_target="tpu_custom_call" | custom-call | flops 2000000000 | bytes 4194304 | tf_op jit(solution)/shard_map/own/pallas_call | solution.py:603
  69.1 3.0 %collective-permute-done.11.refs_5_ = f32[384,640]{1,0:T(8,128)S(1)} collective-permute-done((f32[384,640]{1,0:T(8,128)S(1)}, f32[384,640]{1,0:T(8,128)S(1)}, u32[]{:S(2)}, u32[]{:S(2)}) %collective-permute-start.11) | collective-permute-done | bytes 983072 | tf_op jit(solution)/shard_map/ppermute | solution.py:27
  72.1 0.7 collective-permute-start.15
  72.8 0.1 slice.9.refs_0_
  72.9 1.8 %collective-permute-done.14.refs_7_ = f32[384,640]{1,0:T(8,128)S(1)} collective-permute-done((f32[384,640]{1,0:T(8,128)S(1)}, f32[384,640]{1,0:T(8,128)S(1)}, u32[]{:S(2)}, u32[]{:S(2)}) %collective-permute-start.14) | collective-permute-done | bytes 983072 | tf_op jit(solution)/shard_map/ppermute | solution.py:27
  74.7 17.3 %parent.1 = (f32[512,128]{1,0:T(8,128)}, f32[512,3968]{1,0:T(8,128)}) custom-call(s32[8,12]{1,0:T(8,128)S(1)} %bitcast.10, f32[2,512,512]{2,1,0:T(8,128)S(1)} %corner_second.1.refs_4_.refs_1_, f32[4096,128]{1,0:T(8,128)S(1)} %get-tuple-element.44.refs_2_, f32[640,4096]{1,0:T(8,128)S(1)} %get-tuple-element.45.refs_3_, f32[384,640]{1,0:T(8,128)S(1)} %slice.8.refs_4_, ...), custom_call_target="tpu_custom_call" | custom-call | flops 2000000000 | bytes 4194304 | tf_op jit(solution)/shard_map/parent/pallas_call | solution.py:618
  92.0 0.1 collective-permute-done.15.refs_2_
  92.1 4.0 %far.1 = f32[512,3968]{1,0:T(8,128)} custom-call(s32[8,12]{1,0:T(8,128)S(1)} %bitcast.11, f32[384,384]{1,0:T(8,128)S(1)} %slice.9.refs_0_, f32[384,512]{1,0:T(8,128)S(1)} %collective-permute-done.12.refs_1_, f32[384,512]{1,0:T(8,128)S(1)} %collective-permute-done.15.refs_2_, f32[512,3968]{1,0:T(8,128)} %get-tuple-element.54.refs_3_), custom_call_target="tpu_custom_call", output_to_operand_aliasing={{}: (4, {})} | custom-call | flops 2000000000 | bytes 4194304 | tf_op jit(solution)/shard_map/far/pallas_call | solution.py:637
  (25 shorter events, 0.1 us)
Async XLA Ops:
  3.1 20.1 %copy-start.7 = (f32[136,512]{1,0:T(8,128)S(1)}, f32[136,512]{1,0:T(8,128)}, u32[]{:S(2)}) copy-start(f32[136,512]{1,0:T(8,128)} %get-tuple-element.30) | copy-start | bytes 835588
  3.1 23.2 %copy-start.2 = (f32[136,512]{1,0:T(8,128)S(1)}, f32[136,512]{1,0:T(8,128)}, u32[]{:S(2)}) copy-start(f32[136,512]{1,0:T(8,128)} %get-tuple-element.29.refs_0_.refs_3_) | copy-start | bytes 835588
  3.1 9.9 %collective-permute-start.3 = (f32[136,512]{1,0:T(8,128)}, f32[136,512]{1,0:T(8,128)S(1)}, u32[]{:S(2)}, u32[]{:S(2)}) collective-permute-start(f32[136,512]{1,0:T(8,128)} %get-tuple-element.30), channel_id=1, source_target_pairs={{0,4},{4,0},{8,12},{12,8},{16,20},{20,16},{24,28},{28,24},{1,5},{5... | collective-permute-start | bytes 835592 | tf_op jit(solution)/shard_map/ppermute | solution.py:32
  6.2 8.3 %collective-permute-start = (f32[136,512]{1,0:T(8,128)}, f32[136,512]{1,0:T(8,128)S(1)}, u32[]{:S(2)}, u32[]{:S(2)}) collective-permute-start(f32[136,512]{1,0:T(8,128)} %get-tuple-element.30), channel_id=1, source_target_pairs={{0,2},{1,3},{2,0},{3,1},{4,6},{5,7},{6,4},{7,5},{8,10},{9,11},{10,... | collective-permute-start | bytes 835592 | tf_op jit(solution)/shard_map/ppermute | solution.py:27
  14.5 7.2 %collective-permute-start.4 = (f32[136,512]{1,0:T(8,128)S(1)}, f32[136,512]{1,0:T(8,128)S(1)}, u32[]{:S(2)}, u32[]{:S(2)}) collective-permute-start(f32[136,512]{1,0:T(8,128)S(1)} %collective-permute-done.3.refs_4_), channel_id=1, source_target_pairs={{0,2},{1,3},{2,0},{3,1},{4,6},{5,7},{6,4},{7,5},{8,10},{9,11},{10,... | collective-permute-start | bytes 835592 | tf_op jit(solution)/shard_map/ppermute | solution.py:27
  16.0 34.9 %collective-permute-start.7 = (f32[384,1024]{1,0:T(8,128)}, f32[384,1024]{1,0:T(8,128)S(1)}, u32[]{:S(2)}, u32[]{:S(2)}) collective-permute-start(f32[384,1024]{1,0:T(8,128)} %get-tuple-element.37), channel_id=1, source_target_pairs={{0,4},{4,0},{8,12},{12,8},{16,20},{20,16},{24,28},{28,24},{1,5},{5... | collective-permute-start | bytes 4718600 | tf_op jit(solution)/shard_map/ppermute | solution.py:32
  21.7 25.1 %collective-permute-start.9 = (f32[384,640]{1,0:T(8,128)}, f32[384,640]{1,0:T(8,128)S(1)}, u32[]{:S(2)}, u32[]{:S(2)}) collective-permute-start(f32[384,640]{1,0:T(8,128)} %get-tuple-element.39.refs_6_), channel_id=1, source_target_pairs={{0,2},{1,3},{2,0},{3,1},{4,6},{5,7},{6,4},{7,5},{8,10},{9,11},{10,... | collective-permute-start | bytes 2949128 | tf_op jit(solution)/shard_map/ppermute | solution.py:27
  23.2 1.6 %collective-permute-start.1 = (f32[136,512]{1,0:T(8,128)S(1)}, f32[136,512]{1,0:T(8,128)S(1)}, u32[]{:S(2)}, u32[]{:S(2)}) collective-permute-start(f32[136,512]{1,0:T(8,128)S(1)} %copy-done.7), channel_id=1, source_target_pairs={{0,1},{1,0},{2,3},{3,2},{4,5},{5,4},{6,7},{7,6},{8,9},{9,8},{10,11... | collective-permute-start | bytes 835592 | tf_op jit(solution)/shard_map/ppermute | solution.py:27
  23.2 2.4 %collective-permute-start.5 = (f32[136,512]{1,0:T(8,128)S(1)}, f32[136,512]{1,0:T(8,128)S(1)}, u32[]{:S(2)}, u32[]{:S(2)}) collective-permute-start(f32[136,512]{1,0:T(8,128)S(1)} %collective-permute-done.3.refs_4_), channel_id=1, source_target_pairs={{0,1},{1,0},{2,3},{3,2},{4,5},{5,4},{6,7},{7,6},{8,9},{9,8},{10,11... | collective-permute-start | bytes 835592 | tf_op jit(solution)/shard_map/ppermute | solution.py:27
  23.7 1.8 %collective-permute-start.2 = (f32[136,512]{1,0:T(8,128)S(1)}, f32[136,512]{1,0:T(8,128)S(1)}, u32[]{:S(2)}, u32[]{:S(2)}) collective-permute-start(f32[136,512]{1,0:T(8,128)S(1)} %collective-permute-done.refs_1_), channel_id=1, source_target_pairs={{0,1},{1,0},{2,3},{3,2},{4,5},{5,4},{6,7},{7,6},{8,9},{9,8},{10,11... | collective-permute-start | bytes 835592 | tf_op jit(solution)/shard_map/ppermute | solution.py:27
  24.7 1.6 %collective-permute-start.6 = (f32[136,512]{1,0:T(8,128)S(1)}, f32[136,512]{1,0:T(8,128)S(1)}, u32[]{:S(2)}, u32[]{:S(2)}) collective-permute-start(f32[136,512]{1,0:T(8,128)S(1)} %collective-permute-done.4.refs_5_), channel_id=1, source_target_pairs={{0,1},{1,0},{2,3},{3,2},{4,5},{5,4},{6,7},{7,6},{8,9},{9,8},{10,11... | collective-permute-start | bytes 835592 | tf_op jit(solution)/shard_map/ppermute | solution.py:27
  26.3 20.2 %copy-start.1 = (f32[384,640]{1,0:T(8,128)S(1)}, f32[384,640]{1,0:T(8,128)}, u32[]{:S(2)}) copy-start(f32[384,640]{1,0:T(8,128)} %get-tuple-element.39.refs_6_) | copy-start | bytes 2949124
  26.3 25.2 %copy-start.6 = (f32[384,512]{1,0:T(8,128)S(1)}, f32[384,512]{1,0:T(8,128)}, u32[]{:S(2)}) copy-start(f32[384,512]{1,0:T(8,128)} %get-tuple-element.48) | copy-start | bytes 2359300
  46.5 5.7 %collective-permute-start.8 = (f32[384,640]{1,0:T(8,128)S(1)}, f32[384,640]{1,0:T(8,128)S(1)}, u32[]{:S(2)}, u32[]{:S(2)}) collective-permute-start(f32[384,640]{1,0:T(8,128)S(1)} %copy-done.1), channel_id=1, source_target_pairs={{0,1},{1,0},{2,3},{3,2},{4,5},{5,4},{6,7},{7,6},{8,9},{9,8},{10,11... | collective-permute-start | bytes 2949128 | tf_op jit(solution)/shard_map/ppermute | solution.py:27
  46.7 5.5 %collective-permute-start.10 = (f32[384,640]{1,0:T(8,128)S(1)}, f32[384,640]{1,0:T(8,128)S(1)}, u32[]{:S(2)}, u32[]{:S(2)}) collective-permute-start(f32[384,640]{1,0:T(8,128)S(1)} %collective-permute-done.9.refs_7_), channel_id=1, source_target_pairs={{0,1},{1,0},{2,3},{3,2},{4,5},{5,4},{6,7},{7,6},{8,9},{9,8},{10,11... | collective-permute-start | bytes 2949128 | tf_op jit(solution)/shard_map/ppermute | solution.py:27
  50.9 21.2 %collective-permute-start.11 = (f32[384,640]{1,0:T(8,128)S(1)}, f32[384,640]{1,0:T(8,128)S(1)}, u32[]{:S(2)}, u32[]{:S(2)}) collective-permute-start(f32[384,640]{1,0:T(8,128)S(1)} %slice.8.refs_4_), channel_id=1, source_target_pairs={{0,2},{1,3},{2,0},{3,1},{4,6},{5,7},{6,4},{7,5},{8,10},{9,11},{10,... | collective-permute-start | bytes 2949128 | tf_op jit(solution)/shard_map/ppermute | solution.py:27
  51.5 17.6 %collective-permute-start.12 = (f32[384,512]{1,0:T(8,128)S(1)}, f32[384,512]{1,0:T(8,128)S(1)}, u32[]{:S(2)}, u32[]{:S(2)}) collective-permute-start(f32[384,512]{1,0:T(8,128)S(1)} %copy-done.6), channel_id=1, source_target_pairs={{0,4},{4,0},{8,12},{12,8},{16,20},{20,16},{24,28},{28,24},{1,5},{5... | collective-permute-start | bytes 2359304 | tf_op jit(solution)/shard_map/ppermute | solution.py:32
  52.2 5.9 %copy-start = (f32[1,1,512,2048]{3,2,1,0:T(8,128)S(1)}, f32[1,1,512,2048]{3,2,1,0:T(8,128)}, u32[]{:S(2)}) copy-start(f32[1,1,512,2048]{3,2,1,0:T(8,128)} %param.3) | copy-start | bytes 12582916
  52.2 5.9 %copy-start.3 = (s32[8,1,12]{2,1,0:T(1,128)S(1)}, s32[8,1,12]{2,1,0:T(1,128)}, u32[]{:S(2)}) copy-start(s32[8,1,12]{2,1,0:T(1,128)} %param.5) | copy-start | bytes 1156
  52.2 5.9 %copy-start.4 = (f32[1,1,512]{2,1,0:T(1,128)S(1)}, f32[1,1,512]{2,1,0:T(1,128)}, u32[]{:S(2)}) copy-start(f32[1,1,512]{2,1,0:T(1,128)} %param.4) | copy-start | bytes 6148
  58.2 13.9 %copy-start.5 = (f32[384,512]{1,0:T(8,128)S(1)}, f32[384,512]{1,0:T(8,128)}, u32[]{:S(2)}) copy-start(f32[384,512]{1,0:T(8,128)} %get-tuple-element.53) | copy-start | bytes 2359300
  69.1 3.7 %collective-permute-start.13 = (f32[384,640]{1,0:T(8,128)S(1)}, f32[384,640]{1,0:T(8,128)S(1)}, u32[]{:S(2)}, u32[]{:S(2)}) collective-permute-start(f32[384,640]{1,0:T(8,128)S(1)} %slice.8.refs_4_), channel_id=1, source_target_pairs={{0,1},{1,0},{2,3},{3,2},{4,5},{5,4},{6,7},{7,6},{8,9},{9,8},{10,11... | collective-permute-start | bytes 2949128 | tf_op jit(solution)/shard_map/ppermute | solution.py:27
  72.1 2.6 %collective-permute-start.14 = (f32[384,640]{1,0:T(8,128)S(1)}, f32[384,640]{1,0:T(8,128)S(1)}, u32[]{:S(2)}, u32[]{:S(2)}) collective-permute-start(f32[384,640]{1,0:T(8,128)S(1)} %collective-permute-done.11.refs_5_), channel_id=1, source_target_pairs={{0,1},{1,0},{2,3},{3,2},{4,5},{5,4},{6,7},{7,6},{8,9},{9,8},{10,11... | collective-permute-start | bytes 2949128 | tf_op jit(solution)/shard_map/ppermute | solution.py:27
  72.1 20.0 %collective-permute-start.15 = (f32[384,512]{1,0:T(8,128)S(1)}, f32[384,512]{1,0:T(8,128)S(1)}, u32[]{:S(2)}, u32[]{:S(2)}) collective-permute-start(f32[384,512]{1,0:T(8,128)S(1)} %copy-done.5), channel_id=1, source_target_pairs={{0,4},{4,0},{8,12},{12,8},{16,20},{20,16},{24,28},{28,24},{1,5},{5... | collective-permute-start | bytes 2359304 | tf_op jit(solution)/shard_map/ppermute | solution.py:32
